TPU v7x, 32 devices: a whole 2x2x4 slice. The times are simulated.
32 devices in a mesh: groups: 2 (over y), slab: 4 (over z), dp: 4 (over x, core).
Axes of the slice: x: 2, y: 2, z: 4, core: 2. Of those that a mesh axis runs over, the one named last changes fastest.
Arguments:
- lattice_field: bfloat16 [8, 64, 8, 1024], P(('groups', 'dp'), None, 'slab'), parts along dimension 0, may hold values from -6 to 6
- fine_kernels: bfloat16 [2, 32, 32, 3, 3], P(None, 'dp'), may hold values from -0.375 to 0.375
- coarse_kernels: bfloat16 [2, 8, 8, 3, 3], P(None, 'dp'), may hold values from -0.75 to 0.75
Outputs:
- fine_latent: float32 [8, 64, 8, 1024], P(('groups', 'dp'), None, 'slab'), parts along dimension 0
- coarse_latent: float32 [8, 16, 4, 512], P(('groups', 'dp'), None, 'slab'), parts along dimension 0
- neg_log_density: float32 [8], P(('groups', 'dp')), parts along dimension 0
- fine_grads: float32 [4, 32, 32, 3, 3], P('groups', 'dp'), parts along dimension 0
- coarse_grads: float32 [4, 8, 8, 3, 3], P('groups', 'dp'), parts along dimension 0
There are 2 independent parts, one for each index of `groups`. A program takes and returns all parts, laid end to end along the dimension named above; an argument that names none is the same for every part. Nothing has to cross between parts.
All inputs are finite; a program needn't handle non-finite values.
Results may differ from a plain program's by a relative error of at most 0.0025.
Values may be sent and summed in bfloat16 or wider, within the bound.
A program may use at most 128 MiB of HBM per device.

v0:
```python
import jax
import jax.numpy as jnp
from jax import lax
from jax.sharding import PartitionSpec as P

CC = 16


FORWARD_NUMBERS = ("NCHW", "OIHW", "NCHW")


def padded_2(block, sides, width):
    for axis, dim in sides:
        count = lax.axis_size(axis)
        forward = [(i, i + 1) for i in range(count - 1)]
        forward.append((count - 1, 0))
        backward = [(target, source) for source, target in forward]
        low = lax.ppermute(
            lax.slice_in_dim(block, block.shape[dim] - width, None, axis=dim), axis, forward
        )
        high = lax.ppermute(lax.slice_in_dim(block, 0, width, axis=dim), axis, backward)
        block = jnp.concatenate([low, block, high], axis=dim)
    return block


def correlate(padded, kernel):
    return lax.conv_general_dilated(
        padded,
        kernel,
        (1, 1),
        "VALID",
        dimension_numbers=FORWARD_NUMBERS,
        preferred_element_type=jnp.float32,
    )


def spread_back(slope, kernel):
    widened = jnp.pad(slope, ((0, 0), (0, 0), (2, 2), (2, 2)))
    flipped = jnp.transpose(kernel[:, :, ::-1, ::-1], (1, 0, 2, 3))
    return correlate(widened, flipped)


def kernel_term(padded, slope):
    row_count, col_count = (slope.shape[2], slope.shape[3])
    stacked_rows = []
    for offset_row in range(3):
        row_terms = [
            jnp.einsum(
                "bcij,boij->oc",
                padded[
                    :, :, offset_row : offset_row + row_count, offset_col : offset_col + col_count
                ],
                slope,
                preferred_element_type=jnp.float32,
            )
            for offset_col in range(3)
        ]
        stacked_rows.append(jnp.stack(row_terms, axis=-1))
    return jnp.stack(stacked_rows, axis=-2)


def wrap_both(condition):
    return jnp.pad(condition, ((0, 0), (0, 0), (1, 1), (1, 1)), mode="wrap")


def fold_wrap(gradient):
    interior = gradient[:, :, :, 1:-1]
    interior = (
        interior.at[:, :, :, 0].add(gradient[:, :, :, -1]).at[:, :, :, -1].add(gradient[:, :, :, 0])
    )
    trimmed = interior[:, :, 1:-1]
    return trimmed.at[:, :, 0].add(interior[:, :, -1]).at[:, :, -1].add(interior[:, :, 0])


def wrap_columns(with_rows):
    return jnp.concatenate([with_rows[..., -1:], with_rows, with_rows[..., :1]], axis=3)


def fold_columns(gradient):
    interior = gradient[..., 1:-1]
    return interior.at[..., 0].add(gradient[..., -1]).at[..., -1].add(gradient[..., 0])


def rim_pair(gradient):
    return jnp.concatenate([gradient[:, :, :1], gradient[:, :, -1:]], axis=2)


def fold_rims(gradient, outside):
    interior = gradient[:, :, 1:-1]
    interior = interior.at[:, :, 0].add(outside[:, :, 0])
    return interior.at[:, :, -1].add(outside[:, :, 3])


def fine_widener(condition):
    with_rows = padded_2(condition, (("slab", 2),), 1)
    return wrap_columns(with_rows)


def fine_narrower(gradient):
    folded = fold_columns(gradient)
    outside = padded_2(rim_pair(folded), (("slab", 2),), 1)
    return fold_rims(folded, outside)


def couple(current, kernel, layer_index, widener):
    half_count = current.shape[1] // 2
    if layer_index % 2 == 0:
        condition, moving = (current[:, :half_count], current[:, half_count:])
    else:
        condition, moving = (current[:, half_count:], current[:, :half_count])
    padded = widener(condition.astype(jnp.bfloat16))
    bent_part = jnp.tanh(correlate(padded, kernel))
    moving = moving + bent_part
    if layer_index % 2 == 0:
        joined = jnp.concatenate([condition, moving], axis=1)
    else:
        joined = jnp.concatenate([moving, condition], axis=1)
    return (joined, (padded, bent_part))


def uncouple(gradient, kernel, layer_index, stored, narrower):
    padded, bent_part = stored
    half_count = gradient.shape[1] // 2
    if layer_index % 2 == 0:
        grad_cond, grad_moving = (gradient[:, :half_count], gradient[:, half_count:])
    else:
        grad_cond, grad_moving = (gradient[:, half_count:], gradient[:, :half_count])
    slope = (grad_moving * (1.0 - bent_part * bent_part)).astype(jnp.bfloat16)
    grad_cond = grad_cond + narrower(spread_back(slope, kernel))
    kernel_grad = kernel_term(padded, slope)
    if layer_index % 2 == 0:
        joined = jnp.concatenate([grad_cond, grad_moving], axis=1)
    else:
        joined = jnp.concatenate([grad_moving, grad_cond], axis=1)
    return (joined, kernel_grad)


def pool_field(current, channel_count):
    lattice_count, _, row_count, col_count = current.shape
    return 0.5 * current[:, :channel_count].reshape(
        lattice_count, channel_count, row_count // 2, 2, col_count // 2, 2
    ).sum(axis=(3, 5))


def unpool_field(gradient):
    return 0.5 * jnp.repeat(jnp.repeat(gradient, 2, axis=2), 2, axis=3)


def on_device(lattice_field, fine_kernels, coarse_kernels):
    site_count = lattice_field.shape[2] * lax.axis_size("slab") * lattice_field.shape[3]
    fine_layers = fine_kernels.shape[0]
    coarse_layers = coarse_kernels.shape[0]

    def fine_panel(layer_index):
        return lax.all_gather(fine_kernels[layer_index], "dp", axis=0, tiled=True)

    def coarse_panel(layer_index):
        return lax.all_gather(coarse_kernels[layer_index], "dp", axis=0, tiled=True)

    current = lattice_field.astype(jnp.float32)
    fine_stored = []
    for layer_index in range(fine_layers):
        current, stored = couple(current, fine_panel(layer_index), layer_index, fine_widener)
        fine_stored.append(stored)
    pooled = pool_field(current, CC)
    own_count = pooled.shape[2]
    source = lax.all_gather(pooled, "slab", axis=2, tiled=True)
    widener, narrower = (wrap_both, fold_wrap)
    row_start = lax.axis_index("slab") * own_count
    coarse_current = source
    coarse_stored = []
    for layer_index in range(coarse_layers):
        coarse_current, stored = couple(
            coarse_current, coarse_panel(layer_index), layer_index, widener
        )
        coarse_stored.append(stored)
    coarse_own = lax.dynamic_slice_in_dim(coarse_current, row_start, own_count, 2)
    density_part = (
        0.5
        * (
            jnp.sum(current * current, axis=(1, 2, 3))
            - jnp.sum(pooled * pooled, axis=(1, 2, 3))
            + jnp.sum(coarse_own * coarse_own, axis=(1, 2, 3))
        )
        / site_count
    )
    gradient = coarse_current / site_count
    coarse_list = [None] * coarse_layers
    for layer_index in reversed(range(coarse_layers)):
        gradient, kernel_grad = uncouple(
            gradient, coarse_panel(layer_index), layer_index, coarse_stored[layer_index], narrower
        )
        coarse_list[layer_index] = kernel_grad
    gradient = lax.dynamic_slice_in_dim(gradient, row_start, own_count, 2)
    pooled_grad = gradient - pooled / site_count
    gradient = (current / site_count).at[:, :CC].add(unpool_field(pooled_grad))
    fine_list = [None] * fine_layers
    for layer_index in reversed(range(fine_layers)):
        gradient, kernel_grad = uncouple(
            gradient, fine_panel(layer_index), layer_index, fine_stored[layer_index], fine_narrower
        )
        fine_list[layer_index] = kernel_grad
    fine_share, coarse_share = (
        lax.psum_scatter(jnp.stack(fine_list), "dp", scatter_dimension=1, tiled=True),
        lax.psum_scatter(jnp.stack(coarse_list), "dp", scatter_dimension=1, tiled=True),
    )
    fine_share, density = lax.psum((fine_share, density_part), "slab")
    return (current, coarse_own, density, fine_share, coarse_share)


def solution(mesh):
    in_specs = (
        P(("groups", "dp"), None, "slab", None),
        P(None, "dp", None, None, None),
        P(None, "dp", None, None, None),
    )
    out_specs = (
        P(("groups", "dp"), None, "slab", None),
        P(("groups", "dp"), None, "slab", None),
        P(("groups", "dp")),
        P("groups", "dp", None, None, None),
        P("groups", "dp", None, None, None),
    )
    return jax.shard_map(
        on_device, mesh=mesh, in_specs=in_specs, out_specs=out_specs, check_vma=False
    )
```

profile of v0, /device:TPU:0, one launch (start us, length us, event | category | flops | bytes accessed | tf_op | source)
XLA Modules:
  0.0 180.8 jit_solution(14679561923712001187)
XLA Ops:
  7.2 1.0 copy_convert_fusion
  8.3 3.1 %collective-permute-start = (bf16[1,32,1,1024]{3,1,2,0:T(8,128)(2,1)S(1)}, bf16[1,32,1,1024]{3,1,2,0:T(8,128)(2,1)S(1)}, u32[]{:S(2)}, u32[]{:S(2)}) collective-permute-start(bf16[1,32,1,1024]{3,1,2,0:T(8,128)(2,1)S(1)} %get-tuple-element.228), channel_id=1, source_target_pairs={{0,4},{4,8},{8,12},{12,0},{1,5},{5,9},{9,13},{13,1},{2,6},{6,10},{... | collective-permute-start | bytes 196616 | tf_op jit(solution)/shard_map/ppermute | solution.py:18
  11.4 2.1 %collective-permute-start.1 = (bf16[1,32,1,1024]{3,1,2,0:T(8,128)(2,1)S(1)}, bf16[1,32,1,1024]{3,1,2,0:T(8,128)(2,1)S(1)}, u32[]{:S(2)}, u32[]{:S(2)}) collective-permute-start(bf16[1,32,1,1024]{3,1,2,0:T(8,128)(2,1)S(1)} %get-tuple-element.229), channel_id=1, source_target_pairs={{4,0},{8,4},{12,8},{0,12},{5,1},{9,5},{13,9},{1,13},{6,2},{10,6},{... | collective-permute-start | bytes 196616 | tf_op jit(solution)/shard_map/ppermute | solution.py:21
  14.8 5.6 %all-gather.3 = bf16[1,8,8,3,3]{2,4,3,0,1:T(4,128)(2,1)} all-gather(bf16[1,2,8,3,3]{2,4,3,0,1:T(4,128)(2,1)S(1)} %copy.223), channel_id=5, replica_groups=mesh['groups'=2,'slab'=4,'dp'=4] {'dp'}, dimensions={1}, use_global_device_ids=true | all-gather | bytes 1440 | tf_op jit(solution)/shard_map/all_gather | solution.py:158
  20.4 5.6 %all-gather.4 = bf16[1,8,8,3,3]{2,4,3,0,1:T(4,128)(2,1)} all-gather(bf16[1,2,8,3,3]{2,4,3,0,1:T(4,128)(2,1)S(1)} %copy.224), channel_id=6, replica_groups=mesh['groups'=2,'slab'=4,'dp'=4] {'dp'}, dimensions={1}, use_global_device_ids=true | all-gather | bytes 1440 | tf_op jit(solution)/shard_map/all_gather | solution.py:158
  26.0 5.3 %all-gather = bf16[1,32,32,3,3]{2,1,4,3,0:T(8,128)(2,1)S(1)} all-gather(bf16[1,8,32,3,3]{2,1,4,3,0:T(8,128)(2,1)S(1)} %get-tuple-element.239), channel_id=2, replica_groups=mesh['groups'=2,'slab'=4,'dp'=4] {'dp'}, dimensions={1}, use_global_device_ids=true | all-gather | bytes 23040 | tf_op jit(solution)/shard_map/all_gather | solution.py:155
  31.3 5.3 %all-gather.1 = bf16[1,32,32,3,3]{2,1,4,3,0:T(8,128)(2,1)S(1)} all-gather(bf16[1,8,32,3,3]{2,1,4,3,0:T(8,128)(2,1)S(1)} %get-tuple-element.238), channel_id=3, replica_groups=mesh['groups'=2,'slab'=4,'dp'=4] {'dp'}, dimensions={1}, use_global_device_ids=true | all-gather | bytes 23040 | tf_op jit(solution)/shard_map/all_gather | solution.py:155
  37.7 1.1 copy.175
  38.8 1.1 fusion.8
  42.1 3.8 %collective-permute-start.3 = (bf16[1,32,1,1024]{3,1,2,0:T(8,128)(2,1)S(1)}, bf16[1,32,1,1024]{3,1,2,0:T(8,128)(2,1)S(1)}, u32[]{:S(2)}, u32[]{:S(2)}) collective-permute-start(bf16[1,32,1,1024]{3,1,2,0:T(8,128)(2,1)S(1)} %get-tuple-element.227), channel_id=1, source_target_pairs={{4,0},{8,4},{12,8},{0,12},{5,1},{9,5},{13,9},{1,13},{6,2},{10,6},{... | collective-permute-start | bytes 196616 | tf_op jit(solution)/shard_map/ppermute | solution.py:21
  45.9 0.9 maximum_maximum_fusion
  47.1 0.9 reshape.809
  50.3 1.1 copy.179
  51.4 1.1 fusion.12
  53.0 1.0 multiply_subtract_fusion
  56.1 22.6 %all-gather.2 = f32[16,2048]{0,1:T(8,128)S(1)} all-gather(f32[16,512]{0,1:T(8,128)S(1)} %get-tuple-element.217), channel_id=4, replica_groups=mesh['groups'=2,'slab'=4,'dp'=4] {'slab'}, dimensions={1}, use_global_device_ids=true | all-gather | bytes 163840 | tf_op jit(solution)/shard_map/all_gather | solution.py:167
  80.9 0.9 copy-done.6
  81.8 3.0 %fusion.23 = f32[4,8,65,8]{3,1,2,0:T(8,128)S(1)} fusion(bf16[8,6,1,7,2]{0,3,4,1,2:T(8,128)(2,1)S(1)} %slice.772, bf16[8,6,1,8,65]{0,3,4,1,2:T(8,128)(2,1)} %copy-done.6, bf16[1,8,8,3,3]{2,4,3,0,1:T(4,128)(2,1)} %all-gather.3), kind=kOutput, calls=%fused_computation.28 | convolution fusion | flops 2550528 | bytes 118976 | tf_op jit(solution)/shard_map/conv_general_dilated | solution.py:27
  84.9 1.1 copy.190
  85.9 1.6 multiply_subtract_fusion.3
  88.9 1.9 %fusion.27 = f32[4,8,65,8]{3,1,2,0:T(8,128)S(1)} fusion(bf16[8,6,1,7,2]{0,3,4,1,2:T(8,128)(2,1)S(1)} %slice.776, bf16[8,6,1,8,65]{0,3,4,1,2:T(8,128)(2,1)S(1)} %copy.193, bf16[1,8,8,3,3]{2,4,3,0,1:T(4,128)(2,1)S(1)} %copy-done.36), kind=kOutput, calls=%fused_computation.31 | convolution fusion | flops 2550528 | bytes 118976 | tf_op jit(solution)/shard_map/conv_general_dilated | solution.py:27
  93.3 3.2 %convolution_select_fusion.2 = f32[6,8,65,8]{3,1,2,0:T(8,128)S(1)} fusion(pred[8,65]{0,1:T(8,128)(4,1)S(1)} %copy-done.44, bf16[8,4,1,7,2]{0,3,4,1,2:T(8,128)(2,1)S(1)} %slice.782, bf16[8,4,1,8,65]{0,3,4,1,2:T(8,128)(2,1)} %copy-done.18, bf16[1,8,8,3,3]{2,4,3,0,1:T(4,128)(2,1)S(1)} %copy-done.37), kind=kOutput, calls=%fused_computation.8 | convolution fusion | flops 2524032 | bytes 135688 | tf_op jit(solution)/shard_map/conv_general_dilated | solution.py:27
  102.6 3.2 %convolution_select_fusion.1 = f32[6,8,65,8]{3,1,2,0:T(8,128)S(1)} fusion(pred[8,65]{0,1:T(8,128)(4,1)S(1)} %copy-done.45, bf16[8,4,1,7,2]{0,3,4,1,2:T(8,128)(2,1)S(1)} %slice.795, bf16[8,4,1,8,65]{0,3,4,1,2:T(8,128)(2,1)} %copy-done.17, bf16[1,8,8,3,3]{2,4,3,0,1:T(4,128)(2,1)S(1)} %copy-done.35), kind=kOutput, calls=%fused_computation.7 | convolution fusion | flops 2524032 | bytes 135688 | tf_op jit(solution)/shard_map/conv_general_dilated | solution.py:27
  108.6 1.5 broadcast_multiply_fusion
  111.7 3.1 %convolution_select_fusion = f32[4,8,129,32]{3,1,2,0:T(8,128)} fusion(pred[8,129]{0,1:T(8,128)(4,1)S(1)} %copy-done.42, bf16[32,2,1,7,2]{0,3,4,1,2:T(8,128)(2,1)S(1)} %slice.810, bf16[32,2,1,8,129]{0,3,4,1,2:T(8,128)(2,1)S(1)} %copy.211, bf16[1,32,32,3,3]{2,1,4,3,0:T(8,128)(2,1)S(1)} %copy-done.33), kind=kOutput, calls=%fused_computation.6 | convolution fusion | flops 38578176 | bytes 681736 | tf_op jit(solution)/shard_map/conv_general_dilated | solution.py:27
  114.7 2.6 %copy.212 = f32[4,8,129,32]{2,1,3,0:T(8,128)S(1)} copy(f32[4,8,129,32]{3,1,2,0:T(8,128)} %convolution_select_fusion) | data formatting | bytes 1056768 | tf_op jit(solution)/shard_map/conv_general_dilated | solution.py:27
  120.7 3.8 %collective-permute-start.5 = (f32[1,32,1,1024]{3,1,2,0:T(8,128)S(1)}, f32[1,32,1,1024]{3,1,2,0:T(8,128)S(1)}, u32[]{:S(2)}, u32[]{:S(2)}) collective-permute-start(f32[1,32,1,1024]{3,1,2,0:T(8,128)S(1)} %get-tuple-element.207), channel_id=1, source_target_pairs={{4,0},{8,4},{12,8},{0,12},{5,1},{9,5},{13,9},{1,13},{6,2},{10,6},{... | collective-permute-start | bytes 393224 | tf_op jit(solution)/shard_map/ppermute | solution.py:21
  125.0 2.5 %collective-permute-done.4 = f32[1,32,1,1024]{3,1,2,0:T(8,128)S(1)} collective-permute-done((f32[1,32,1,1024]{3,1,2,0:T(8,128)S(1)}, f32[1,32,1,1024]{3,1,2,0:T(8,128)S(1)}, u32[]{:S(2)}, u32[]{:S(2)}) %collective-permute-start.4) | collective-permute-done | bytes 131104 | tf_op jit(solution)/shard_map/ppermute | solution.py:18
  131.6 1.2 copy.214
  134.7 10.9 %all-reduce = f32[2,8,8,3,3]{2,1,4,3,0:T(8,128)S(1)} all-reduce(f32[2,8,8,3,3]{2,1,4,3,0:T(8,128)S(1)} %pad_maximum_fusion.11), channel_id=8, replica_groups=mesh['groups'=2,'slab'=4,'dp'=4] {'dp'}, use_global_device_ids=true, to_apply=%region_8.9.clone | all-reduce | flops 1152 | bytes 9216
  146.2 6.1 %reduce-scatter.3.cloned.1.call-done = f32[2,8,32,3,3]{2,1,4,3,0:T(8,128)} async-done(((f32[2,32,32,3,3]{2,1,4,3,0:T(8,128)}), f32[2,8,32,3,3]{2,1,4,3,0:T(8,128)}) %reduce-scatter.3.cloned.1.call-update) | async-done | bytes 18448 | tf_op jit(solution)/shard_map/reduce_scatter | solution.py:204
  152.3 21.6 %all-reduce.1 = (f32[1]{0:T(128)}, f32[2,8,32,3,3]{2,1,4,3,0:T(8,128)}) all-reduce(f32[1]{0:T(128)} %bitcast.18, f32[2,8,32,3,3]{2,1,4,3,0:T(8,128)} %reduce-scatter.3.cloned.1.call-done), channel_id=1, replica_groups=mesh['groups'=2,'slab'=4,'dp'=4] {'slab'}, use_global_device_ids=true, to_apply=%region_5.6 | all-reduce | flops 4609 | bytes 36872 | tf_op jit(solution)/shard_map/psum | solution.py:207
  (279 shorter events, 33.5 us)
Async XLA Ops:
  7.2 6.4 %copy-start.43 = (u32[32]{0:T(128)S(1)}, u32[32]{0:T(128)}, u32[]{:S(2)}) copy-start(u32[32]{0:T(128)} %constant.385) | copy-start | bytes 388
  7.2 6.3 %copy-start.34 = (bf16[2,8,32,3,3]{2,1,4,3,0:T(8,128)(2,1)S(1)}, bf16[2,8,32,3,3]{2,1,4,3,0:T(8,128)(2,1)}, u32[]{:S(2)}) copy-start(bf16[2,8,32,3,3]{2,1,4,3,0:T(8,128)(2,1)} %param.30) | copy-start | bytes 27652
  7.2 6.3 %copy-start.38 = (bf16[2,2,8,3,3]{2,1,4,3,0:T(2,128)(2,1)S(1)}, bf16[2,2,8,3,3]{2,1,4,3,0:T(2,128)(2,1)}, u32[]{:S(2)}) copy-start(bf16[2,2,8,3,3]{2,1,4,3,0:T(2,128)(2,1)} %param.31) | copy-start | bytes 1732
  7.2 145.1 %reduce-scatter.3.cloned.1.call-start = ((), (), s32[]{:S(2)}) async-start(), calls=%async_computation.1 | async-start | bytes 368640 | tf_op jit(solution)/shard_map/reduce_scatter | solution.py:204
  8.3 28.3 %collective-permute-start = (bf16[1,32,1,1024]{3,1,2,0:T(8,128)(2,1)S(1)}, bf16[1,32,1,1024]{3,1,2,0:T(8,128)(2,1)S(1)}, u32[]{:S(2)}, u32[]{:S(2)}) collective-permute-start(bf16[1,32,1,1024]{3,1,2,0:T(8,128)(2,1)S(1)} %get-tuple-element.228), channel_id=1, source_target_pairs={{0,4},{4,8},{8,12},{12,0},{1,5},{5,9},{9,13},{13,1},{2,6},{6,10},{... | collective-permute-start | bytes 196616 | tf_op jit(solution)/shard_map/ppermute | solution.py:18
  11.4 25.2 %collective-permute-start.1 = (bf16[1,32,1,1024]{3,1,2,0:T(8,128)(2,1)S(1)}, bf16[1,32,1,1024]{3,1,2,0:T(8,128)(2,1)S(1)}, u32[]{:S(2)}, u32[]{:S(2)}) collective-permute-start(bf16[1,32,1,1024]{3,1,2,0:T(8,128)(2,1)S(1)} %get-tuple-element.229), channel_id=1, source_target_pairs={{4,0},{8,4},{12,8},{0,12},{5,1},{9,5},{13,9},{1,13},{6,2},{10,6},{... | collective-permute-start | bytes 196616 | tf_op jit(solution)/shard_map/ppermute | solution.py:21
  36.6 14.8 %copy-start.32 = (bf16[1,32,32,3,3]{2,1,4,3,0:T(8,128)(2,1)}, bf16[1,32,32,3,3]{2,1,4,3,0:T(8,128)(2,1)S(1)}, u32[]{:S(2)}) copy-start(bf16[1,32,32,3,3]{2,1,4,3,0:T(8,128)(2,1)S(1)} %all-gather.1) | copy-start | bytes 55300
  36.6 9.3 %copy-start.7 = (bf16[1,32,1,1024]{3,1,2,0:T(8,128)(2,1)}, bf16[1,32,1,1024]{3,1,2,0:T(8,128)(2,1)S(1)}, u32[]{:S(2)}) copy-start(bf16[1,32,1,1024]{3,1,2,0:T(8,128)(2,1)S(1)} %collective-permute-done) | copy-start | bytes 196612
  36.6 9.3 %copy-start.9 = (bf16[1,32,1,1024]{3,1,2,0:T(8,128)(2,1)}, bf16[1,32,1,1024]{3,1,2,0:T(8,128)(2,1)S(1)}, u32[]{:S(2)}) copy-start(bf16[1,32,1,1024]{3,1,2,0:T(8,128)(2,1)S(1)} %collective-permute-done.1) | copy-start | bytes 196612
  42.0 6.8 %collective-permute-start.2 = (bf16[1,32,1,1024]{3,1,2,0:T(8,128)(2,1)S(1)}, bf16[1,32,1,1024]{3,1,2,0:T(8,128)(2,1)S(1)}, u32[]{:S(2)}, u32[]{:S(2)}) collective-permute-start(bf16[1,32,1,1024]{3,1,2,0:T(8,128)(2,1)S(1)} %get-tuple-element.226), channel_id=1, source_target_pairs={{0,4},{4,8},{8,12},{12,0},{1,5},{5,9},{9,13},{13,1},{2,6},{6,10},{... | collective-permute-start | bytes 196616 | tf_op jit(solution)/shard_map/ppermute | solution.py:18
  42.1 6.7 %collective-permute-start.3 = (bf16[1,32,1,1024]{3,1,2,0:T(8,128)(2,1)S(1)}, bf16[1,32,1,1024]{3,1,2,0:T(8,128)(2,1)S(1)}, u32[]{:S(2)}, u32[]{:S(2)}) collective-permute-start(bf16[1,32,1,1024]{3,1,2,0:T(8,128)(2,1)S(1)} %get-tuple-element.227), channel_id=1, source_target_pairs={{4,0},{8,4},{12,8},{0,12},{5,1},{9,5},{13,9},{1,13},{6,2},{10,6},{... | collective-permute-start | bytes 196616 | tf_op jit(solution)/shard_map/ppermute | solution.py:21
  88.0 2.8 %copy-start.26 = (bf16[1,8,1,512]{3,1,2,0:T(8,128)(2,1)}, bf16[1,8,1,512]{3,1,2,0:T(8,128)(2,1)S(1)}, u32[]{:S(2)}) copy-start(bf16[1,8,1,512]{3,1,2,0:T(8,128)(2,1)S(1)} %get-tuple-element.240) | copy-start | bytes 24580
  88.1 2.7 %copy-start.28 = (bf16[1,8,6,1]{3,1,2,0:T(8,128)(2,1)}, bf16[1,8,6,1]{3,1,2,0:T(8,128)(2,1)S(1)}, u32[]{:S(2)}) copy-start(bf16[1,8,6,1]{3,1,2,0:T(8,128)(2,1)S(1)} %get-tuple-element.234) | copy-start | bytes 292
  88.1 2.7 %copy-start.30 = (bf16[1,8,6,1]{3,1,2,0:T(8,128)(2,1)}, bf16[1,8,6,1]{3,1,2,0:T(8,128)(2,1)S(1)}, u32[]{:S(2)}) copy-start(bf16[1,8,6,1]{3,1,2,0:T(8,128)(2,1)S(1)} %get-tuple-element.235) | copy-start | bytes 292
  91.5 1.7 copy-start.37
  91.5 1.7 copy-start.44
  91.7 1.6 copy-start.15
  96.4 1.6 copy-start.19
  97.0 1.7 copy-start.20
  97.2 2.4 %copy-start.27 = (bf16[1,8,1,512]{3,1,2,0:T(8,128)(2,1)S(1)}, bf16[1,8,1,512]{3,1,2,0:T(8,128)(2,1)}, u32[]{:S(2)}) copy-start(bf16[1,8,1,512]{3,1,2,0:T(8,128)(2,1)} %copy-done.26) | copy-start | bytes 24580
  97.2 2.4 %copy-start.29 = (bf16[1,8,6,1]{3,1,2,0:T(8,128)(2,1)S(1)}, bf16[1,8,6,1]{3,1,2,0:T(8,128)(2,1)}, u32[]{:S(2)}) copy-start(bf16[1,8,6,1]{3,1,2,0:T(8,128)(2,1)} %copy-done.28) | copy-start | bytes 292
  97.2 2.4 %copy-start.31 = (bf16[1,8,6,1]{3,1,2,0:T(8,128)(2,1)S(1)}, bf16[1,8,6,1]{3,1,2,0:T(8,128)(2,1)}, u32[]{:S(2)}) copy-start(bf16[1,8,6,1]{3,1,2,0:T(8,128)(2,1)} %copy-done.30) | copy-start | bytes 292
  98.5 4.1 %copy-start.35 = (bf16[1,8,8,3,3]{2,4,3,0,1:T(4,128)(2,1)S(1)}, bf16[1,8,8,3,3]{2,4,3,0,1:T(4,128)(2,1)}, u32[]{:S(2)}) copy-start(bf16[1,8,8,3,3]{2,4,3,0,1:T(4,128)(2,1)} %all-gather.3) | copy-start | bytes 3460
  98.5 4.1 %copy-start.45 = (pred[8,65]{0,1:T(8,128)(4,1)S(1)}, pred[8,65]{0,1:T(8,128)(4,1)}, u32[]{:S(2)}) copy-start(pred[8,65]{0,1:T(8,128)(4,1)} %constant.380) | copy-start | bytes 1564
  108.0 2.0 %copy-start = (f32[2,8,129,32]{2,3,1,0:T(8,128)S(1)}, f32[2,8,129,32]{2,3,1,0:T(8,128)}, u32[]{:S(2)}) copy-start(f32[2,8,129,32]{2,3,1,0:T(8,128)} %get-tuple-element.205) | copy-start | bytes 792580
  120.6 6.9 %collective-permute-start.4 = (f32[1,32,1,1024]{3,1,2,0:T(8,128)S(1)}, f32[1,32,1,1024]{3,1,2,0:T(8,128)S(1)}, u32[]{:S(2)}, u32[]{:S(2)}) collective-permute-start(f32[1,32,1,1024]{3,1,2,0:T(8,128)S(1)} %get-tuple-element.208), channel_id=1, source_target_pairs={{0,4},{4,8},{8,12},{12,0},{1,5},{5,9},{9,13},{13,1},{2,6},{6,10},{... | collective-permute-start | bytes 393224 | tf_op jit(solution)/shard_map/ppermute | solution.py:18
  120.7 6.9 %collective-permute-start.5 = (f32[1,32,1,1024]{3,1,2,0:T(8,128)S(1)}, f32[1,32,1,1024]{3,1,2,0:T(8,128)S(1)}, u32[]{:S(2)}, u32[]{:S(2)}) collective-permute-start(f32[1,32,1,1024]{3,1,2,0:T(8,128)S(1)} %get-tuple-element.207), channel_id=1, source_target_pairs={{4,0},{8,4},{12,8},{0,12},{5,1},{9,5},{13,9},{1,13},{6,2},{10,6},{... | collective-permute-start | bytes 393224 | tf_op jit(solution)/shard_map/ppermute | solution.py:21
  124.8 2.9 %copy-start.4 = (f32[2,1,1032,32]{2,3,0,1:T(8,128)S(1)}, f32[2,1,1032,32]{2,3,0,1:T(8,128)}, u32[]{:S(2)}) copy-start(f32[2,1,1032,32]{2,3,0,1:T(8,128)} %reshape.809) | copy-start | bytes 792580
  125.0 2.7 %copy-start.3 = (bf16[1,32,4,1025]{3,1,2,0:T(8,128)(2,1)S(1)}, bf16[1,32,4,1025]{3,1,2,0:T(8,128)(2,1)}, u32[]{:S(2)}) copy-start(bf16[1,32,4,1025]{3,1,2,0:T(8,128)(2,1)} %get-tuple-element.212) | copy-start | bytes 787204
  125.0 3.0 %copy-start.2 = (bf16[1,32,4,1025]{3,1,2,0:T(8,128)(2,1)S(1)}, bf16[1,32,4,1025]{3,1,2,0:T(8,128)(2,1)}, u32[]{:S(2)}) copy-start(bf16[1,32,4,1025]{3,1,2,0:T(8,128)(2,1)} %get-tuple-element.213) | copy-start | bytes 787204
  127.9 1.5 copy-start.8
  129.3 2.3 %copy-start.1 = (f32[1,64,2,1024]{3,1,2,0:T(8,128)S(1)}, f32[1,64,2,1024]{3,1,2,0:T(8,128)}, u32[]{:S(2)}) copy-start(f32[1,64,2,1024]{3,1,2,0:T(8,128)} %get-tuple-element.210) | copy-start | bytes 1572868
  (21 other events, 19.1 us)
Sparse Core Ops, SparseCore 0:
  130.5 21.7 reduce-scatter.2
where the time goes:
time: 181 us
  blocking collectives  76.9 us (42%)
  local copies, waits for them, and re-layouts  29.3 us (16%)
  matrix products  22.6 us (12%)
  between operations  17.8 us (10%)
  starting transfers between devices  12.9 us (7%)
  other arithmetic  11.8 us (7%)
  waiting for transfers between devices  9.33 us (5%)
    all_gather x1, blocking collectives, on_device(): source = lax.all_gather(pooled, 'slab', axis=2, tiled=True)  22.6 us
    psum x1, blocking collectives, on_device(): fine_share, density = lax.psum((fine_share, density_part), 'slab')  21.6 us
    conv_general_dilated x7, matrix products, correlate(): lax.conv_general_dilated(padded, kernel, (1, 1), 'VALID', dimension_numbe...  16.4 us
    conv_general_dilated x34, local copies, waits for them, and re-layouts, correlate(): lax.conv_general_dilated(padded, kernel, (1, 1), 'VALID', dimension_numbe...  13.8 us
    all_gather x2, blocking collectives, coarse_panel(): return lax.all_gather(coarse_kernels[layer_index], 'dp', axis=0, tiled=True)  11.2 us
    unnamed x1, blocking collectives  10.9 us
    all_gather x2, blocking collectives, fine_panel(): return lax.all_gather(fine_kernels[layer_index], 'dp', axis=0, tiled=True)  10.6 us
    ppermute x3, starting transfers between devices, padded_2(): lax.ppermute(lax.slice_in_dim(block, 0, width, axis=dim), axis, backward)  9.71 us
  transfers between devices with their start and end apart: 7, of which 3 were waited for; matrix products, arithmetic and copies ran while one was open for 3% of the time, Pallas kernels for 0%

commit v1 on v0

v1 whole, which is shorter than its diff:
```python
import functools

import jax
import jax.numpy as jnp
from jax import lax
from jax.experimental import pallas as pl
from jax.experimental.pallas import tpu as pltpu

MESH = pl.DeviceIdType.MESH
F32 = jnp.float32
BF16 = jnp.bfloat16
LANES = 128


def round_up(value, step):
    return -(-value // step) * step


def product(left, right):
    return jnp.dot(left, right, preferred_element_type=F32)


def product_nt(left, right):
    return lax.dot_general(
        left, right, (((1,), (1,)), ((), ())), preferred_element_type=F32
    )


def columns_forward(rows):
    width = rows.shape[1]
    return jnp.concatenate(
        [pltpu.roll(rows, 1, 1), rows, pltpu.roll(rows, width - 1, 1)], axis=0
    )


def columns_backward(rows):
    width = rows.shape[1]
    return jnp.concatenate(
        [pltpu.roll(rows, width - 1, 1), rows, pltpu.roll(rows, 1, 1)], axis=0
    )


def split_product(value, matrix):
    count = value.shape[0]
    first = value.astype(BF16)
    rest = value - first.astype(F32)
    second = rest.astype(BF16)
    third = (rest - second.astype(F32)).astype(BF16)
    stacked = product(jnp.concatenate([first, second, third], axis=0), matrix)
    return stacked[:count] + stacked[count : 2 * count] + stacked[2 * count :]


def pool_columns(value):
    count, width = value.shape
    blocks = width // 256
    stacked = jnp.concatenate(
        [value[:, 256 * b : 256 * (b + 1)] for b in range(blocks)], axis=0
    )
    source = lax.broadcasted_iota(jnp.int32, (256, 128), 0)
    target = lax.broadcasted_iota(jnp.int32, (256, 128), 1)
    matrix = jnp.where((source >> 1) == target, 0.5, 0.0).astype(BF16)
    summed = split_product(stacked, matrix)
    return jnp.concatenate(
        [summed[count * b : count * (b + 1)] for b in range(blocks)], axis=1
    )


def unpool_columns(value):
    count, width = value.shape
    blocks = width // 128
    stacked = jnp.concatenate(
        [value[:, 128 * b : 128 * (b + 1)] for b in range(blocks)], axis=0
    )
    source = lax.broadcasted_iota(jnp.int32, (128, 256), 0)
    target = lax.broadcasted_iota(jnp.int32, (128, 256), 1)
    matrix = jnp.where((target >> 1) == source, 0.5, 0.0).astype(BF16)
    spread = split_product(stacked, matrix)
    return jnp.concatenate(
        [spread[count * b : count * (b + 1)] for b in range(blocks)], axis=1
    )


def flow_kernel(
    slabs, shards, window, own_fine, own_coarse, site_count,
    x_ref, wa_ref, wb_ref,
    lat_ref, coarse_ref, dens_ref, ga_ref, gb_ref,
    wa_buf, wb_buf, halo0, halo1, c1_ref, tiles0, tiles1, tilesb,
    bend0, bend1, pool_buf, slope_ref, shalo,
    sa_ref, sb_ref, ra_buf, rb_buf, aa_buf, ab_buf,
    send_sem, recv_sem,
):
    half = x_ref.shape[1] // 2
    deep = wb_ref.shape[0] - 2 * half
    mc = deep // 4
    cc = 2 * mc
    patch = 9 * half
    three = 3 * half
    cpatch = 9 * mc
    inverse = 1.0 / site_count
    me = lax.axis_index("slab")
    mine = lax.axis_index("dp")
    above = lax.rem(me + slabs - 1, slabs)
    below = lax.rem(me + 1, slabs)

    barrier = pltpu.get_barrier_semaphore()
    for step in range(1, slabs):
        pl.semaphore_signal(
            barrier, inc=1, device_id={"slab": lax.rem(me + step, slabs)}, device_id_type=MESH
        )
    for step in range(1, shards):
        pl.semaphore_signal(
            barrier, inc=1, device_id={"dp": lax.rem(mine + step, shards)}, device_id_type=MESH
        )
    pl.semaphore_wait(barrier, slabs + shards - 2)

    used = [0]
    started = []

    def send(source, target, device):
        index = used[0]
        used[0] += 1
        copy = pltpu.make_async_remote_copy(
            src_ref=source,
            dst_ref=target,
            send_sem=send_sem.at[index],
            recv_sem=recv_sem.at[index],
            device_id=device,
            device_id_type=MESH,
        )
        copy.start()
        started.append(copy)
        return copy

    wa_copies, wb_copies = [], []
    for step in range(1, shards):
        peer = lax.rem(mine + step, shards)
        wa_copies.append(send(wa_ref, wa_buf.at[step - 1], {"dp": peer}))
    from_above = send(x_ref.at[1, 0:half], halo0.at[0], {"slab": below})
    from_below = send(x_ref.at[0, 0:half], halo0.at[1], {"slab": above})
    for step in range(1, shards):
        peer = lax.rem(mine + step, shards)
        wb_copies.append(send(wb_ref, wb_buf.at[step - 1], {"dp": peer}))

    sa_ref[...] = jnp.zeros_like(sa_ref)
    sb_ref[...] = jnp.zeros_like(sb_ref)

    def set_tile(tiles, index, rows, turn):
        tiles[three * index : three * (index + 1), :] = turn(rows).astype(BF16)

    for i in range(2):
        set_tile(tiles0, i + 1, x_ref[i, 0:half].astype(F32), columns_forward)
    total = wa_ref[...].astype(F32)
    for step in range(1, shards):
        wa_copies[step - 1].wait_recv()
        total = total + wa_buf[step - 1].astype(F32)
    weight0 = total[:, 0:patch].astype(BF16)
    from_above.wait_recv()
    set_tile(tiles0, 0, halo0[0].astype(F32), columns_forward)
    from_below.wait_recv()
    set_tile(tiles0, 3, halo0[1].astype(F32), columns_forward)
    density = jnp.zeros((half, x_ref.shape[2]), F32)
    for i in range(2):
        bent = jnp.tanh(product(weight0, tiles0[three * i : three * i + patch, :]))
        moved = x_ref[i, half:].astype(F32) + bent
        lat_ref[i, half:] = moved
        bend0[i] = 1.0 - bent * bent
        c1_ref[i] = moved.astype(BF16)
    from_above = send(c1_ref.at[1], halo1.at[0], {"slab": below})
    from_below = send(c1_ref.at[0], halo1.at[1], {"slab": above})

    for i in range(2):
        set_tile(tiles1, i + 1, c1_ref[i].astype(F32), columns_forward)
        moved = lat_ref[i, half:]
        density = density + moved * moved
    total = wb_ref[...].astype(F32)
    for step in range(1, shards):
        wb_copies[step - 1].wait_recv()
        total = total + wb_buf[step - 1].astype(F32)
    weights = total.astype(BF16)
    weight1 = weights[0:half, 0:patch]
    back1 = weights[half : 2 * half, 0:patch]
    coarse_weights = total[2 * half :, 0:cpatch]
    cfor0, cfor1, cback1, cback0 = [
        coarse_weights[mc * k : mc * (k + 1)].astype(BF16) for k in range(4)
    ]
    from_above.wait_recv()
    set_tile(tiles1, 0, halo1[0].astype(F32), columns_forward)
    from_below.wait_recv()
    set_tile(tiles1, 3, halo1[1].astype(F32), columns_forward)
    for i in range(2):
        bent = jnp.tanh(product(weight1, tiles1[three * i : three * i + patch, :]))
        moved = x_ref[i, 0:half].astype(F32) + bent
        lat_ref[i, 0:half] = moved
        bend1[i] = 1.0 - bent * bent
        density = density + moved * moved

    pool_buf[0] = pool_columns(lat_ref[0, 0:cc] + lat_ref[1, 0:cc])
    pool_copies = []
    for k in range(1, window):
        offset = k if k <= window // 2 else k - window
        peer = lax.rem(me - offset + slabs, slabs)
        pool_copies.append(send(pool_buf.at[0], pool_buf.at[k], {"slab": peer}))
    for i in range(2):
        slope_ref[i, cc:half] = (lat_ref[i, cc:half] * inverse * bend1[i, cc:half]).astype(BF16)
    high_above = send(slope_ref.at[1, cc:half], shalo.at[0, cc:half], {"slab": below})
    high_below = send(slope_ref.at[0, cc:half], shalo.at[1, cc:half], {"slab": above})
    for copy in pool_copies:
        copy.wait_recv()

    width = pool_buf.shape[2]

    def coarse_patches(rows, turn, sign, wanted):
        turned = [turn(row) for row in rows]
        columns = []
        for k in wanted:
            near = [turned[(k + sign * (p - 1)) % window] for p in range(3)]
            columns.append(jnp.concatenate(near, axis=0))
        return jnp.concatenate(columns, axis=1).astype(BF16)

    def cut(value):
        return [value[:, width * k : width * (k + 1)] for k in range(value.shape[1] // width)]

    def rounded(value):
        return value.astype(BF16).astype(F32)

    everything = range(window)
    low = jnp.concatenate([pool_buf[k, 0:mc] for k in everything], axis=1)
    high = jnp.concatenate([pool_buf[k, mc:cc] for k in everything], axis=1)
    patches0 = coarse_patches(cut(rounded(low)), columns_forward, 1, everything)
    bent_c0 = jnp.tanh(product(cfor0, patches0))
    high = high + bent_c0
    patches1 = coarse_patches(cut(rounded(high)), columns_forward, 1, everything)
    bent_c1 = jnp.tanh(product(cfor1, patches1))
    low = low + bent_c1
    coarse_own = jnp.concatenate([low[:, 0:width], high[:, 0:width]], axis=0)
    coarse_ref[...] = coarse_own
    pooled = pool_buf[0]

    grad_low = low * inverse
    slope_c1 = (grad_low * (1.0 - bent_c1 * bent_c1)).astype(BF16)
    kernel_c1 = product_nt(slope_c1[:, 0:width], patches1[:, 0:width])
    back_patches = coarse_patches(cut(slope_c1.astype(F32)), columns_backward, -1, everything)
    grad_high = high * inverse + product(cback1, back_patches)
    slope_c0 = (grad_high * (1.0 - bent_c0 * bent_c0)).astype(BF16)
    kernel_c0 = product_nt(slope_c0[:, 0:width], patches0[:, 0:width])
    back_patches = coarse_patches(cut(slope_c0.astype(F32)), columns_backward, -1, [0])
    grad_own = grad_low[:, 0:width] + product(cback0, back_patches)
    pooled_grad = jnp.concatenate([grad_own, grad_high[:, 0:width]], axis=0) - pooled * inverse
    spread = unpool_columns(pooled_grad)

    for i in range(2):
        slope_ref[i, 0:cc] = ((lat_ref[i, 0:cc] * inverse + spread) * bend1[i, 0:cc]).astype(BF16)
    low_above = send(slope_ref.at[1, 0:cc], shalo.at[0, 0:cc], {"slab": below})
    low_below = send(slope_ref.at[0, 0:cc], shalo.at[1, 0:cc], {"slab": above})
    kernel_1 = product_nt(slope_ref[0], tiles1[0:patch, :])
    kernel_1 = kernel_1 + product_nt(slope_ref[1], tiles1[three : three + patch, :])
    pad_fine = round_up(own_fine, 8)
    for d in range(shards):
        sb_ref[d, 0:own_fine, 0:patch] = kernel_1[own_fine * d : own_fine * (d + 1)]
        sb_ref[d, pad_fine : pad_fine + own_coarse, 0:cpatch] = kernel_c0[
            own_coarse * d : own_coarse * (d + 1)
        ]
        sb_ref[d, pad_fine + own_coarse : pad_fine + 2 * own_coarse, 0:cpatch] = kernel_c1[
            own_coarse * d : own_coarse * (d + 1)
        ]
    rb_copies = []
    for step in range(1, shards):
        peer = lax.rem(mine + step, shards)
        rb_copies.append(send(sb_ref.at[peer], rb_buf.at[step - 1], {"dp": peer}))
    for i in range(2):
        set_tile(tilesb, 2 - i, slope_ref[i].astype(F32), columns_backward)

    folded = density[0:8]
    for b in range(1, half // 8):
        folded = folded + density[8 * b : 8 * (b + 1)]
    narrow = folded[:, 0:width] + folded[:, width:]
    for b in range(cc // 8):
        part = slice(8 * b, 8 * (b + 1))
        narrow = narrow - pooled[part] * pooled[part] + coarse_own[part] * coarse_own[part]
    tile = narrow[:, 0:LANES]
    for b in range(1, width // LANES):
        tile = tile + narrow[:, LANES * b : LANES * (b + 1)]
    tile = tile * (0.5 * inverse)

    high_above.wait_recv()
    low_above.wait_recv()
    set_tile(tilesb, 3, shalo[0].astype(F32), columns_backward)
    high_below.wait_recv()
    low_below.wait_recv()
    set_tile(tilesb, 0, shalo[1].astype(F32), columns_backward)
    kernel_0 = None
    for i in range(2):
        start = three * (1 - i)
        grad = lat_ref[i, half:] * inverse + product(back1, tilesb[start : start + patch, :])
        slope = (grad * bend0[i]).astype(BF16)
        term = product_nt(slope, tiles0[three * i : three * i + patch, :])
        kernel_0 = term if kernel_0 is None else kernel_0 + term
    for d in range(shards):
        sa_ref[d, 0:own_fine, 0:patch] = kernel_0[own_fine * d : own_fine * (d + 1)]
    ra_copies = []
    for step in range(1, shards):
        peer = lax.rem(mine + step, shards)
        ra_copies.append(send(sa_ref.at[peer], ra_buf.at[step - 1], {"dp": peer}))

    def over_slabs(gathered):
        copies = []
        for step in range(1, slabs):
            peer = lax.rem(me + step, slabs)
            copies.append(used[0])
            send(gathered.at[me], gathered.at[me], {"slab": peer})
        return copies

    block = sb_ref[mine]
    for step in range(1, shards):
        rb_copies[step - 1].wait_recv()
        block = block + rb_buf[step - 1]
    rows_b = sb_ref.shape[1]
    ab_buf[me, 0:rows_b] = block
    ab_buf[me, rows_b:] = jnp.concatenate(
        [tile, jnp.zeros((8, ab_buf.shape[2] - LANES), F32)], axis=1
    )
    ab_copies = over_slabs(ab_buf)
    block = sa_ref[mine]
    for step in range(1, shards):
        ra_copies[step - 1].wait_recv()
        block = block + ra_buf[step - 1]
    aa_buf[me] = block
    aa_copies = over_slabs(aa_buf)

    def wait_slabs(gathered, copies):
        for step in range(1, slabs):
            source = lax.rem(me - step + slabs, slabs)
            pltpu.make_async_remote_copy(
                src_ref=gathered.at[me],
                dst_ref=gathered.at[source],
                send_sem=send_sem.at[copies[step - 1]],
                recv_sem=recv_sem.at[copies[step - 1]],
                device_id={"slab": source},
                device_id_type=MESH,
            ).wait_recv()

    wait_slabs(ab_buf, ab_copies)
    block = ab_buf[0]
    for s in range(1, slabs):
        block = block + ab_buf[s]
    gb_ref[...] = block[0:rows_b]
    dens_ref[...] = jnp.broadcast_to(jnp.sum(block[rows_b:, 0:LANES], keepdims=True), (8, LANES))
    wait_slabs(aa_buf, aa_copies)
    block = aa_buf[0]
    for s in range(1, slabs):
        block = block + aa_buf[s]
    ga_ref[...] = block
    for copy in started:
        copy.wait_send()


def on_device(lattice_field, fine_kernels, coarse_kernels):
    slabs, shards = lax.axis_size("slab"), lax.axis_size("dp")
    mine = lax.axis_index("dp")
    _, channels, height, cols = lattice_field.shape
    _, own_fine, half, _, _ = fine_kernels.shape
    _, own_coarse, mc, _, _ = coarse_kernels.shape
    cc, width = 2 * mc, cols // 2
    patch, cpatch = 9 * half, 9 * mc
    padded = round_up(patch, LANES)
    site_count = height * slabs * cols
    window = min(slabs, 9)

    def embedded(kernel, own):
        count = own * shards
        tiled = jnp.tile(kernel, (1, shards, 1, 1, 1))
        owner = lax.broadcasted_iota(jnp.int32, (1, count, 1, 1, 1), 1) // own
        full = jnp.where(owner == mine, tiled, jnp.zeros_like(tiled))
        forward = jnp.transpose(full, (0, 1, 3, 4, 2)).reshape(2, count, -1)
        backward = jnp.transpose(full, (0, 2, 3, 4, 1)).reshape(2, count, -1)
        pads = ((0, 0), (0, 0), (0, padded - forward.shape[2]))
        return jnp.pad(forward, pads), jnp.pad(backward, pads)

    forward, backward = embedded(fine_kernels, own_fine)
    cforward, cbackward = embedded(coarse_kernels, own_coarse)
    wa = forward[0]
    wb = jnp.concatenate(
        [forward[1], backward[1], cforward[0], cforward[1], cbackward[1], cbackward[0]], axis=0
    )
    x = jnp.transpose(lattice_field[0], (1, 0, 2))

    pad_fine = round_up(own_fine, 8)
    rows_b = pad_fine + 8
    copies = 4 * (shards - 1) + 8 + (window - 1) + 2 * (slabs - 1)
    vmem = pl.BlockSpec(memory_space=pltpu.VMEM)
    lat, coarse, dens, ga, gb = pl.pallas_call(
        functools.partial(
            flow_kernel, slabs, shards, window, own_fine, own_coarse, site_count
        ),
        out_shape=(
            jax.ShapeDtypeStruct((2, channels, cols), F32),
            jax.ShapeDtypeStruct((cc, width), F32),
            jax.ShapeDtypeStruct((8, LANES), F32),
            jax.ShapeDtypeStruct((pad_fine, padded), F32),
            jax.ShapeDtypeStruct((rows_b, padded), F32),
        ),
        in_specs=[vmem] * 3,
        out_specs=(vmem,) * 5,
        scratch_shapes=[
            pltpu.VMEM((shards - 1,) + wa.shape, BF16),
            pltpu.VMEM((shards - 1,) + wb.shape, BF16),
            pltpu.VMEM((2, half, cols), BF16),
            pltpu.VMEM((2, half, cols), BF16),
            pltpu.VMEM((2, half, cols), BF16),
            pltpu.VMEM((12 * half, cols), BF16),
            pltpu.VMEM((12 * half, cols), BF16),
            pltpu.VMEM((12 * half, cols), BF16),
            pltpu.VMEM((2, half, cols), F32),
            pltpu.VMEM((2, half, cols), F32),
            pltpu.VMEM((window, cc, width), F32),
            pltpu.VMEM((2, half, cols), BF16),
            pltpu.VMEM((2, half, cols), BF16),
            pltpu.VMEM((shards, pad_fine, padded), F32),
            pltpu.VMEM((shards, rows_b, padded), F32),
            pltpu.VMEM((shards - 1, pad_fine, padded), F32),
            pltpu.VMEM((shards - 1, rows_b, padded), F32),
            pltpu.VMEM((slabs, pad_fine, padded), F32),
            pltpu.VMEM((slabs, rows_b + 8, padded), F32),
            pltpu.SemaphoreType.DMA((copies,)),
            pltpu.SemaphoreType.DMA((copies,)),
        ],
        compiler_params=pltpu.CompilerParams(
            collective_id=0, has_side_effects=True, vmem_limit_bytes=40 * 1024 * 1024
        ),
    )(x, wa, wb)

    def unfold(rows, own, count):
        return jnp.transpose(rows.reshape(own, 3, 3, count), (0, 3, 1, 2))

    fine = jnp.stack(
        [
            unfold(ga[0:own_fine, 0:patch], own_fine, half),
            unfold(gb[0:own_fine, 0:patch], own_fine, half),
        ]
    )
    coarse_rows = gb[pad_fine : pad_fine + 2 * own_coarse, 0:cpatch]
    coarse_grads = jnp.stack(
        [
            unfold(coarse_rows[0:own_coarse], own_coarse, mc),
            unfold(coarse_rows[own_coarse:], own_coarse, mc),
        ]
    )
    return (
        jnp.transpose(lat, (1, 0, 2))[None],
        coarse[None, :, None, :],
        dens[0, 0:1],
        fine,
        coarse_grads,
    )


def solution(mesh):
    from jax.sharding import PartitionSpec as P

    in_specs = (
        P(("groups", "dp"), None, "slab", None),
        P(None, "dp", None, None, None),
        P(None, "dp", None, None, None),
    )
    out_specs = (
        P(("groups", "dp"), None, "slab", None),
        P(("groups", "dp"), None, "slab", None),
        P(("groups", "dp")),
        P("groups", "dp", None, None, None),
        P("groups", "dp", None, None, None),
    )
    return jax.shard_map(
        on_device, mesh=mesh, in_specs=in_specs, out_specs=out_specs, check_vma=False
    )
```

time: 181 us -> 40.3 us (0.22)
  blocking collectives: 76.9 us -> 0 us
  Pallas kernels: 0 us -> 33 us
  local copies, waits for them, and re-layouts: 29.3 us -> 6.05 us
  matrix products: 22.6 us -> 0 us
  between operations: 17.8 us -> 0.78 us
  starting transfers between devices: 12.9 us -> 0 us
  other arithmetic: 11.8 us -> 0.3 us
  waiting for transfers between devices: 9.33 us -> 0 us
    all_gather x5 -> x0, blocking collectives: 44.4 us -> none  [the longest x1 22.6 us: on_device(): source = lax.all_gather(pooled, 'slab', axis=2, tiled=True)]
    pallas_call x0 -> x1, Pallas kernels: none -> 33 us  [on_device(): pl.pallas_call(functools.partial(flow_kernel, slabs, shards, window, own_...]
    psum x1 -> x0, blocking collectives: 21.6 us -> none  [on_device(): fine_share, density = lax.psum((fine_share, density_part), 'slab')]
    conv_general_dilated x7 -> x0, matrix products: 16.4 us -> none  [correlate(): lax.conv_general_dilated(padded, kernel, (1, 1), 'VALID', dimension_numbe...]
    conv_general_dilated x34 -> x0, local copies, waits for them, and re-layouts: 13.8 us -> none  [correlate(): lax.conv_general_dilated(padded, kernel, (1, 1), 'VALID', dimension_numbe...]
    ppermute x6 -> x0, starting transfers between devices: 12.9 us -> none  [the longest x3 9.71 us: padded_2(): lax.ppermute(lax.slice_in_dim(block, 0, width, axis=dim), axis, backward)]
    unnamed x1 -> x0, blocking collectives: 10.9 us -> none
    dot_general x36 -> x0, matrix products: 6.26 us -> none  [kernel_term(): jnp.einsum('bcij,boij->oc', padded[:, :, offset_row:offset_row + row_coun...]
  transfers between devices with their start and end apart: 7 -> 0, of which waited for: 3 -> 0; matrix products, arithmetic and copies ran while one was open for 3% -> 0% of each run, Pallas kernels for 0% -> 0%
where the time goes in v1:
time: 40.3 us; the launch traced here: 40.1 us
  Pallas kernels  33 us (82%)
  local copies, waits for them, and re-layouts  6.05 us (15%)
  between operations  0.78 us (2%)
    pallas_call x1, Pallas kernels, on_device(): pl.pallas_call(functools.partial(flow_kernel, slabs, shards, window, own_...  33 us
    unnamed x16, local copies, waits for them, and re-layouts  4.56 us

profile of v1, /device:TPU:0, one launch (start us, length us, event | category | flops | bytes accessed | tf_op | source)
XLA Modules:
  0.0 40.1 jit_solution(10740278906131672348)
XLA Ops:
  0.6 0.0 copy-start.2
  0.6 0.0 copy-start
  0.7 0.7 %copy-done.2 = bf16[2,2,8,3,3]{2,1,4,3,0:T(2,128)(2,1)S(1)} copy-done((bf16[2,2,8,3,3]{2,1,4,3,0:T(2,128)(2,1)S(1)}, bf16[2,2,8,3,3]{2,1,4,3,0:T(2,128)(2,1)}, u32[]{:S(2)}) %copy-start.2) | copy-done | bytes 600
  1.4 0.1 fusion.13
  1.4 0.1 broadcast_select_fusion
  1.5 0.1 copy.29
  1.6 0.1 reshape.122
  1.7 0.0 copy-done
  1.7 0.0 copy-start.1
  1.8 0.7 %copy-done.1 = bf16[2,8,32,3,3]{2,1,4,3,0:T(8,128)(2,1)S(1)} copy-done((bf16[2,8,32,3,3]{2,1,4,3,0:T(8,128)(2,1)S(1)}, bf16[2,8,32,3,3]{2,1,4,3,0:T(8,128)(2,1)}, u32[]{:S(2)}) %copy-start.1) | copy-done | bytes 9240
  2.5 0.1 bitcast_select_fusion
  2.6 0.1 copy.28
  2.7 0.1 copy.20
  2.8 0.1 reshape.120
  3.1 33.0 %shard_map.74 = (f32[2,64,1024]{2,1,0:T(8,128)S(1)}, f32[16,512]{1,0:T(8,128)S(1)}, f32[8,128]{1,0:T(8,128)S(1)}, f32[8,384]{1,0:T(8,128)S(1)}, f32[16,384]{1,0:T(8,128)S(1)}) custom-call(bf16[2,64,1024]{2,1,0:T(8,128)(2,1)S(1)} %bitcast.64, bf16[32,384]{1,0:T(8,128)(2,1)S(1)} %fusion.wa_ref, bf16[96,384]{1,0:T(8,128)(2,1)S(1)} %constant_dynamic-update-slice_fusion.wb_ref), custom_call_target="tpu_custom_call" | custom-call | tf_op jit(solution)/shard_map/pallas_call | solution.py:391
  36.0 0.5 %slice.46 = f32[1,1]{1,0:T(1,128)} slice(f32[8,128]{1,0:T(8,128)S(1)} %get-tuple-element.12), slice={[0:1], [0:1]} | slice | bytes 8 | tf_op jit(solution)/shard_map/slice | solution.py:451
  36.6 1.2 %copy.24 = f32[1,64,2,1024]{3,2,1,0:T(2,128)} copy(f32[1,64,2,1024]{3,1,2,0:T(8,128)S(1)} %bitcast.65) | data formatting | bytes 1048576
  37.8 0.6 %copy.25 = f32[1,16,1,512]{3,2,1,0:T(1,128)} copy(f32[1,16,1,512]{3,1,2,0:T(8,128)S(1)} %bitcast.66) | data formatting | bytes 65536
  38.4 0.1 reshape.126
  38.5 0.1 reshape.127
  38.6 0.6 %copy.27 = f32[2,2,8,3,3]{2,1,4,3,0:T(2,128)} copy(f32[2,2,8,3,3]{2,4,3,1,0:T(4,128)S(1)} %pad_maximum_fusion.1) | data formatting | bytes 2304
  39.2 0.1 reshape.125
  39.3 0.1 reshape.124
  39.4 0.6 %copy.26 = f32[2,8,32,3,3]{2,1,4,3,0:T(8,128)} copy(f32[2,8,32,3,3]{2,4,3,1,0:T(4,128)S(1)} %pad_maximum_fusion) | data formatting | bytes 36864
  (16 shorter events, 0.2 us)
Async XLA Ops:
  0.6 0.7 %copy-start.2 = (bf16[2,2,8,3,3]{2,1,4,3,0:T(2,128)(2,1)S(1)}, bf16[2,2,8,3,3]{2,1,4,3,0:T(2,128)(2,1)}, u32[]{:S(2)}) copy-start(bf16[2,2,8,3,3]{2,1,4,3,0:T(2,128)(2,1)} %param.5) | copy-start | bytes 1732
  0.6 1.1 %copy-start = (bf16[1,64,2,1024]{3,2,1,0:T(2,128)(2,1)S(1)}, bf16[1,64,2,1024]{3,2,1,0:T(2,128)(2,1)}, u32[]{:S(2)}) copy-start(bf16[1,64,2,1024]{3,2,1,0:T(2,128)(2,1)} %param.3) | copy-start | bytes 786436
  1.7 0.8 %copy-start.1 = (bf16[2,8,32,3,3]{2,1,4,3,0:T(8,128)(2,1)S(1)}, bf16[2,8,32,3,3]{2,1,4,3,0:T(8,128)(2,1)}, u32[]{:S(2)}) copy-start(bf16[2,8,32,3,3]{2,1,4,3,0:T(8,128)(2,1)} %param.4) | copy-start | bytes 27652

commit v2 on v1

--- a/solution.py
+++ b/solution.py
@@ -83,9 +83,9 @@
 def flow_kernel(
     slabs, shards, window, own_fine, own_coarse, site_count,
     x_ref, wa_ref, wb_ref,
-    lat_ref, coarse_ref, dens_ref, ga_ref, gb_ref,
+    out_ref, coarse_ref, dens_ref, fine_ref, cgrad_ref,
     wa_buf, wb_buf, halo0, halo1, c1_ref, tiles0, tiles1, tilesb,
-    bend0, bend1, pool_buf, slope_ref, shalo,
+    lat_ref, bend0, bend1, pool_buf, slope_ref, shalo,
     sa_ref, sb_ref, ra_buf, rb_buf, aa_buf, ab_buf,
     send_sem, recv_sem,
 ):
@@ -96,6 +96,8 @@
     patch = 9 * half
     three = 3 * half
     cpatch = 9 * mc
+    tail = patch // LANES * LANES
+    inset = patch - tail
     inverse = 1.0 / site_count
     me = lax.axis_index("slab")
     mine = lax.axis_index("dp")
@@ -147,24 +149,33 @@
     def set_tile(tiles, index, rows, turn):
         tiles[three * index : three * (index + 1), :] = turn(rows).astype(BF16)
 
+    def own_terms(weight, tiles, first, second):
+        stacked = jnp.concatenate(
+            [weight[:, first : first + 2 * three], weight[:, second : second + 2 * three]], axis=0
+        ).astype(BF16)
+        both = product(stacked, tiles[three : 3 * three, :])
+        return both[0:half], both[half:]
+
     for i in range(2):
         set_tile(tiles0, i + 1, x_ref[i, 0:half].astype(F32), columns_forward)
     total = wa_ref[...].astype(F32)
     for step in range(1, shards):
         wa_copies[step - 1].wait_recv()
         total = total + wa_buf[step - 1].astype(F32)
-    weight0 = total[:, 0:patch].astype(BF16)
+    sums = own_terms(total, tiles0, three, 0)
+    edges = [total[:, 0:three].astype(BF16), total[:, 2 * three : patch].astype(BF16)]
     from_above.wait_recv()
     set_tile(tiles0, 0, halo0[0].astype(F32), columns_forward)
     from_below.wait_recv()
     set_tile(tiles0, 3, halo0[1].astype(F32), columns_forward)
     density = jnp.zeros((half, x_ref.shape[2]), F32)
     for i in range(2):
-        bent = jnp.tanh(product(weight0, tiles0[three * i : three * i + patch, :]))
+        edge = three * 3 * i
+        bent = jnp.tanh(sums[i] + product(edges[i], tiles0[edge : edge + three, :]))
         moved = x_ref[i, half:].astype(F32) + bent
+        c1_ref[i] = moved.astype(BF16)
         lat_ref[i, half:] = moved
         bend0[i] = 1.0 - bent * bent
-        c1_ref[i] = moved.astype(BF16)
     from_above = send(c1_ref.at[1], halo1.at[0], {"slab": below})
     from_below = send(c1_ref.at[0], halo1.at[1], {"slab": above})
 
@@ -176,9 +187,10 @@
     for step in range(1, shards):
         wb_copies[step - 1].wait_recv()
         total = total + wb_buf[step - 1].astype(F32)
-    weights = total.astype(BF16)
-    weight1 = weights[0:half, 0:patch]
-    back1 = weights[half : 2 * half, 0:patch]
+    weight1 = total[0:half]
+    back1 = total[half : 2 * half]
+    sums = own_terms(weight1, tiles1, three, 0)
+    edges = [weight1[:, 0:three].astype(BF16), weight1[:, 2 * three : patch].astype(BF16)]
     coarse_weights = total[2 * half :, 0:cpatch]
     cfor0, cfor1, cback1, cback0 = [
         coarse_weights[mc * k : mc * (k + 1)].astype(BF16) for k in range(4)
@@ -187,12 +199,18 @@
     set_tile(tiles1, 0, halo1[0].astype(F32), columns_forward)
     from_below.wait_recv()
     set_tile(tiles1, 3, halo1[1].astype(F32), columns_forward)
-    for i in range(2):
-        bent = jnp.tanh(product(weight1, tiles1[three * i : three * i + patch, :]))
-        moved = x_ref[i, 0:half].astype(F32) + bent
-        lat_ref[i, 0:half] = moved
-        bend1[i] = 1.0 - bent * bent
-        density = density + moved * moved
+    sums = [
+        sums[i] + product(edges[i], tiles1[three * 3 * i : three * (3 * i + 1), :])
+        for i in range(2)
+    ]
+
+    def finish(part):
+        for i in range(2):
+            bent = jnp.tanh(sums[i][part])
+            lat_ref[i, part] = x_ref[i, part].astype(F32) + bent
+            bend1[i, part] = 1.0 - bent * bent
+
+    finish(slice(0, cc))
 
     pool_buf[0] = pool_columns(lat_ref[0, 0:cc] + lat_ref[1, 0:cc])
     pool_copies = []
@@ -200,10 +218,19 @@
         offset = k if k <= window // 2 else k - window
         peer = lax.rem(me - offset + slabs, slabs)
         pool_copies.append(send(pool_buf.at[0], pool_buf.at[k], {"slab": peer}))
+    finish(slice(cc, half))
     for i in range(2):
         slope_ref[i, cc:half] = (lat_ref[i, cc:half] * inverse * bend1[i, cc:half]).astype(BF16)
     high_above = send(slope_ref.at[1, cc:half], shalo.at[0, cc:half], {"slab": below})
     high_below = send(slope_ref.at[0, cc:half], shalo.at[1, cc:half], {"slab": above})
+    tiles = x_ref.shape[2] // LANES
+    for i in range(2):
+        moved = lat_ref[i, 0:half]
+        density = density + moved * moved
+        for b in range(tiles):
+            out_ref[pl.ds(2 * b + i, 2 * half, stride=2 * tiles), :] = lat_ref[
+                i, :, LANES * b : LANES * (b + 1)
+            ]
     for copy in pool_copies:
         copy.wait_recv()
 
@@ -215,7 +242,7 @@
         for k in wanted:
             near = [turned[(k + sign * (p - 1)) % window] for p in range(3)]
             columns.append(jnp.concatenate(near, axis=0))
-        return jnp.concatenate(columns, axis=1).astype(BF16)
+        return jnp.concatenate(columns, axis=1)
 
     def cut(value):
         return [value[:, width * k : width * (k + 1)] for k in range(value.shape[1] // width)]
@@ -227,24 +254,38 @@
     low = jnp.concatenate([pool_buf[k, 0:mc] for k in everything], axis=1)
     high = jnp.concatenate([pool_buf[k, mc:cc] for k in everything], axis=1)
     patches0 = coarse_patches(cut(rounded(low)), columns_forward, 1, everything)
-    bent_c0 = jnp.tanh(product(cfor0, patches0))
+    bent_c0 = jnp.tanh(product(cfor0, patches0.astype(BF16)))
     high = high + bent_c0
     patches1 = coarse_patches(cut(rounded(high)), columns_forward, 1, everything)
-    bent_c1 = jnp.tanh(product(cfor1, patches1))
+    bent_c1 = jnp.tanh(product(cfor1, patches1.astype(BF16)))
     low = low + bent_c1
     coarse_own = jnp.concatenate([low[:, 0:width], high[:, 0:width]], axis=0)
-    coarse_ref[...] = coarse_own
+    for b in range(width // LANES):
+        coarse_ref[pl.ds(b, cc, stride=width // LANES), :] = coarse_own[
+            :, LANES * b : LANES * (b + 1)
+        ]
     pooled = pool_buf[0]
+
+    def coarse_kernel_grad(slope, patches):
+        widened = jnp.concatenate(
+            [
+                jnp.zeros((inset, width), F32),
+                patches[:, 0:width],
+                jnp.zeros((LANES - inset - cpatch, width), F32),
+            ],
+            axis=0,
+        )
+        return product_nt(slope[:, 0:width], widened.astype(BF16))
 
     grad_low = low * inverse
     slope_c1 = (grad_low * (1.0 - bent_c1 * bent_c1)).astype(BF16)
-    kernel_c1 = product_nt(slope_c1[:, 0:width], patches1[:, 0:width])
+    kernel_c1 = coarse_kernel_grad(slope_c1, patches1)
     back_patches = coarse_patches(cut(slope_c1.astype(F32)), columns_backward, -1, everything)
-    grad_high = high * inverse + product(cback1, back_patches)
+    grad_high = high * inverse + product(cback1, back_patches.astype(BF16))
     slope_c0 = (grad_high * (1.0 - bent_c0 * bent_c0)).astype(BF16)
-    kernel_c0 = product_nt(slope_c0[:, 0:width], patches0[:, 0:width])
+    kernel_c0 = coarse_kernel_grad(slope_c0, patches0)
     back_patches = coarse_patches(cut(slope_c0.astype(F32)), columns_backward, -1, [0])
-    grad_own = grad_low[:, 0:width] + product(cback0, back_patches)
+    grad_own = grad_low[:, 0:width] + product(cback0, back_patches.astype(BF16))
     pooled_grad = jnp.concatenate([grad_own, grad_high[:, 0:width]], axis=0) - pooled * inverse
     spread = unpool_columns(pooled_grad)
 
@@ -254,15 +295,13 @@
     low_below = send(slope_ref.at[0, 0:cc], shalo.at[1, 0:cc], {"slab": above})
     kernel_1 = product_nt(slope_ref[0], tiles1[0:patch, :])
     kernel_1 = kernel_1 + product_nt(slope_ref[1], tiles1[three : three + patch, :])
-    pad_fine = round_up(own_fine, 8)
     for d in range(shards):
         sb_ref[d, 0:own_fine, 0:patch] = kernel_1[own_fine * d : own_fine * (d + 1)]
-        sb_ref[d, pad_fine : pad_fine + own_coarse, 0:cpatch] = kernel_c0[
-            own_coarse * d : own_coarse * (d + 1)
-        ]
-        sb_ref[d, pad_fine + own_coarse : pad_fine + 2 * own_coarse, 0:cpatch] = kernel_c1[
-            own_coarse * d : own_coarse * (d + 1)
-        ]
+        for l, kernel_c in enumerate((kernel_c0, kernel_c1)):
+            place = slice(own_coarse * l, own_coarse * (l + 1))
+            sb_ref[d, place, tail:] = (
+                sb_ref[d, place, tail:] + kernel_c[own_coarse * d : own_coarse * (d + 1)]
+            )
     rb_copies = []
     for step in range(1, shards):
         peer = lax.rem(mine + step, shards)
@@ -280,7 +319,9 @@
     tile = narrow[:, 0:LANES]
     for b in range(1, width // LANES):
         tile = tile + narrow[:, LANES * b : LANES * (b + 1)]
-    tile = tile * (0.5 * inverse)
+    site_density = jnp.sum(tile * (0.5 * inverse), keepdims=True)
+    sums = own_terms(back1, tilesb, 0, three)
+    edges = [back1[:, 2 * three : patch].astype(BF16), back1[:, 0:three].astype(BF16)]
 
     high_above.wait_recv()
     low_above.wait_recv()
@@ -290,8 +331,12 @@
     set_tile(tilesb, 0, shalo[1].astype(F32), columns_backward)
     kernel_0 = None
     for i in range(2):
-        start = three * (1 - i)
-        grad = lat_ref[i, half:] * inverse + product(back1, tilesb[start : start + patch, :])
+        edge = three * 3 * (1 - i)
+        grad = (
+            lat_ref[i, half:] * inverse
+            + sums[i]
+            + product(edges[i], tilesb[edge : edge + three, :])
+        )
         slope = (grad * bend0[i]).astype(BF16)
         term = product_nt(slope, tiles0[three * i : three * i + patch, :])
         kernel_0 = term if kernel_0 is None else kernel_0 + term
@@ -314,11 +359,9 @@
     for step in range(1, shards):
         rb_copies[step - 1].wait_recv()
         block = block + rb_buf[step - 1]
-    rows_b = sb_ref.shape[1]
-    ab_buf[me, 0:rows_b] = block
-    ab_buf[me, rows_b:] = jnp.concatenate(
-        [tile, jnp.zeros((8, ab_buf.shape[2] - LANES), F32)], axis=1
-    )
+    row = lax.broadcasted_iota(jnp.int32, block.shape, 0)
+    lane = lax.broadcasted_iota(jnp.int32, block.shape, 1)
+    ab_buf[me] = jnp.where((row == 2 * own_coarse) & (lane == patch), site_density, block)
     ab_copies = over_slabs(ab_buf)
     block = sa_ref[mine]
     for step in range(1, shards):
@@ -343,15 +386,30 @@
     block = ab_buf[0]
     for s in range(1, slabs):
         block = block + ab_buf[s]
-    gb_ref[...] = block[0:rows_b]
-    dens_ref[...] = jnp.broadcast_to(jnp.sum(block[rows_b:, 0:LANES], keepdims=True), (8, LANES))
+    dens_ref[...] = block[2 * own_coarse : 2 * own_coarse + 1, patch : patch + 1]
+    for k in range(9):
+        fine_ref[1, k] = block[0:own_fine, half * k : half * (k + 1)]
+        for l in range(2):
+            cgrad_ref[l, k] = block[
+                own_coarse * l : own_coarse * (l + 1), patch + mc * k : patch + mc * (k + 1)
+            ]
     wait_slabs(aa_buf, aa_copies)
     block = aa_buf[0]
     for s in range(1, slabs):
         block = block + aa_buf[s]
-    ga_ref[...] = block
+    for k in range(9):
+        fine_ref[0, k] = block[0:own_fine, half * k : half * (k + 1)]
     for copy in started:
         copy.wait_send()
+
+
+def store_kernel(*refs):
+    sem = refs[-1]
+    copies = [pltpu.make_async_copy(refs[k], refs[5 + k], sem.at[k]) for k in range(5)]
+    for copy in copies:
+        copy.start()
+    for copy in copies:
+        copy.wait()
 
 
 def on_device(lattice_field, fine_kernels, coarse_kernels):
@@ -385,20 +443,21 @@
     x = jnp.transpose(lattice_field[0], (1, 0, 2))
 
     pad_fine = round_up(own_fine, 8)
-    rows_b = pad_fine + 8
+    tall = channels * height * cols // LANES
     copies = 4 * (shards - 1) + 8 + (window - 1) + 2 * (slabs - 1)
     vmem = pl.BlockSpec(memory_space=pltpu.VMEM)
-    lat, coarse, dens, ga, gb = pl.pallas_call(
+    shapes = (
+        jax.ShapeDtypeStruct((tall, LANES), F32),
+        jax.ShapeDtypeStruct((cc * width // LANES, LANES), F32),
+        jax.ShapeDtypeStruct((1, 1), F32),
+        jax.ShapeDtypeStruct((2, 9, own_fine, half), F32),
+        jax.ShapeDtypeStruct((2, 9, own_coarse, mc), F32),
+    )
+    results = pl.pallas_call(
         functools.partial(
             flow_kernel, slabs, shards, window, own_fine, own_coarse, site_count
         ),
-        out_shape=(
-            jax.ShapeDtypeStruct((2, channels, cols), F32),
-            jax.ShapeDtypeStruct((cc, width), F32),
-            jax.ShapeDtypeStruct((8, LANES), F32),
-            jax.ShapeDtypeStruct((pad_fine, padded), F32),
-            jax.ShapeDtypeStruct((rows_b, padded), F32),
-        ),
+        out_shape=shapes,
         in_specs=[vmem] * 3,
         out_specs=(vmem,) * 5,
         scratch_shapes=[
@@ -410,17 +469,18 @@
             pltpu.VMEM((12 * half, cols), BF16),
             pltpu.VMEM((12 * half, cols), BF16),
             pltpu.VMEM((12 * half, cols), BF16),
+            pltpu.VMEM((2, channels, cols), F32),
             pltpu.VMEM((2, half, cols), F32),
             pltpu.VMEM((2, half, cols), F32),
             pltpu.VMEM((window, cc, width), F32),
             pltpu.VMEM((2, half, cols), BF16),
             pltpu.VMEM((2, half, cols), BF16),
             pltpu.VMEM((shards, pad_fine, padded), F32),
-            pltpu.VMEM((shards, rows_b, padded), F32),
+            pltpu.VMEM((shards, pad_fine, padded), F32),
             pltpu.VMEM((shards - 1, pad_fine, padded), F32),
-            pltpu.VMEM((shards - 1, rows_b, padded), F32),
+            pltpu.VMEM((shards - 1, pad_fine, padded), F32),
             pltpu.VMEM((slabs, pad_fine, padded), F32),
-            pltpu.VMEM((slabs, rows_b + 8, padded), F32),
+            pltpu.VMEM((slabs, pad_fine, padded), F32),
             pltpu.SemaphoreType.DMA((copies,)),
             pltpu.SemaphoreType.DMA((copies,)),
         ],
@@ -429,28 +489,20 @@
         ),
     )(x, wa, wb)
 
-    def unfold(rows, own, count):
-        return jnp.transpose(rows.reshape(own, 3, 3, count), (0, 3, 1, 2))
-
-    fine = jnp.stack(
-        [
-            unfold(ga[0:own_fine, 0:patch], own_fine, half),
-            unfold(gb[0:own_fine, 0:patch], own_fine, half),
-        ]
-    )
-    coarse_rows = gb[pad_fine : pad_fine + 2 * own_coarse, 0:cpatch]
-    coarse_grads = jnp.stack(
-        [
-            unfold(coarse_rows[0:own_coarse], own_coarse, mc),
-            unfold(coarse_rows[own_coarse:], own_coarse, mc),
-        ]
-    )
+    lat, coarse, dens, fine, coarse_grads = pl.pallas_call(
+        store_kernel,
+        out_shape=shapes,
+        in_specs=[vmem] * 5,
+        out_specs=(pl.BlockSpec(memory_space=pl.ANY),) * 5,
+        scratch_shapes=[pltpu.SemaphoreType.DMA((5,))],
+    )(*results)
+    lat = jnp.transpose(lat.reshape(channels, cols // LANES, height, LANES), (0, 2, 1, 3))
     return (
-        jnp.transpose(lat, (1, 0, 2))[None],
-        coarse[None, :, None, :],
-        dens[0, 0:1],
-        fine,
-        coarse_grads,
+        lat.reshape(1, channels, height, cols),
+        coarse.reshape(1, cc, 1, width),
+        dens.reshape(1),
+        jnp.transpose(fine.reshape(2, 3, 3, own_fine, half), (0, 3, 4, 1, 2)),
+        jnp.transpose(coarse_grads.reshape(2, 3, 3, own_coarse, mc), (0, 3, 4, 1, 2)),
     )
 
 

time: 40.3 us -> 42 us (1.042)
  Pallas kernels: 33 us -> 36.1 us
  local copies, waits for them, and re-layouts: 6.05 us -> 4.69 us
    pallas_call x0 -> x1, Pallas kernels: none -> 2.55 us  [on_device(): pl.pallas_call(store_kernel, out_shape=shapes, in_specs=[vmem] * 5, out_s...]
    pallas_call x1, Pallas kernels: 33 us -> 33.5 us  [on_device(): pl.pallas_call(functools.partial(flow_kernel, slabs, shards, window, own_...]
    slice x3 -> x0, local copies, waits for them, and re-layouts: 0.52 us -> none  [the longest x1 0.51 us: on_device(): dens[0, 0:1]]
    unnamed x16 -> x20, local copies, waits for them, and re-layouts: 4.56 us -> 4.08 us
where the time goes in v2:
time: 42 us; the launch traced here: 41.8 us
  Pallas kernels  36.1 us (86%)
  local copies, waits for them, and re-layouts  4.69 us (11%)
  between operations  0.77 us (2%)
    pallas_call x1, Pallas kernels, on_device(): pl.pallas_call(functools.partial(flow_kernel, slabs, shards, window, own_...  33.5 us
    unnamed x20, local copies, waits for them, and re-layouts  4.08 us
    pallas_call x1, Pallas kernels, on_device(): pl.pallas_call(store_kernel, out_shape=shapes, in_specs=[vmem] * 5, out_s...  2.55 us

profile of v2, /device:TPU:0, one launch (start us, length us, event | category | flops | bytes accessed | tf_op | source)
XLA Modules:
  0.0 41.8 jit_solution(1814074675186073725)
XLA Ops:
  0.6 0.0 copy-start.6
  0.6 0.0 copy-start.4
  0.7 0.7 %copy-done.6 = bf16[2,2,8,3,3]{2,1,4,3,0:T(2,128)(2,1)S(1)} copy-done((bf16[2,2,8,3,3]{2,1,4,3,0:T(2,128)(2,1)S(1)}, bf16[2,2,8,3,3]{2,1,4,3,0:T(2,128)(2,1)}, u32[]{:S(2)}) %copy-start.6) | copy-done | bytes 600
  1.4 0.1 fusion.12
  1.4 0.1 broadcast_select_fusion
  1.5 0.1 copy.23
  1.6 0.1 reshape.128
  1.7 0.0 copy-done.4
  1.7 0.0 copy-start.5
  1.8 0.7 %copy-done.5 = bf16[2,8,32,3,3]{2,1,4,3,0:T(8,128)(2,1)S(1)} copy-done((bf16[2,8,32,3,3]{2,1,4,3,0:T(8,128)(2,1)S(1)}, bf16[2,8,32,3,3]{2,1,4,3,0:T(8,128)(2,1)}, u32[]{:S(2)}) %copy-start.5) | copy-done | bytes 9240
  2.5 0.1 bitcast_select_fusion
  2.6 0.1 copy.22
  2.7 0.1 copy.16
  2.8 0.1 reshape.126
  3.1 33.5 %shard_map.74 = (f32[1024,128]{1,0:T(8,128)S(1)}, f32[64,128]{1,0:T(8,128)S(1)}, f32[1,1]{1,0:T(1,128)}, f32[2,9,8,32]{3,2,1,0:T(8,128)S(1)}, f32[2,9,2,8]{3,2,1,0:T(2,128)S(1)}) custom-call(bf16[2,64,1024]{2,1,0:T(8,128)(2,1)S(1)} %bitcast.59, bf16[32,384]{1,0:T(8,128)(2,1)S(1)} %fusion.wa_ref, bf16[96,384]{1,0:T(8,128)(2,1)S(1)} %constant_dynamic-update-slice_fusion.wb_ref), custom_call_target="tpu_custom_call" | custom-call | tf_op jit(solution)/shard_map/pallas_call | solution.py:456
  36.6 0.0 copy-start
  36.6 0.8 %copy-done = f32[1024,128]{1,0:T(8,128)} copy-done((f32[1024,128]{1,0:T(8,128)}, f32[1024,128]{1,0:T(8,128)S(1)}, u32[]{:S(2)}) %copy-start) | copy-done | bytes 524312
  37.4 0.0 copy-start.1
  37.4 0.6 %copy-done.1 = f32[2,9,8,32]{3,2,1,0:T(8,128)} copy-done((f32[2,9,8,32]{3,2,1,0:T(8,128)}, f32[2,9,8,32]{3,2,1,0:T(8,128)S(1)}, u32[]{:S(2)}) %copy-start.1) | copy-done | bytes 18456
  38.0 0.0 copy-start.2
  38.0 0.6 %copy-done.2 = f32[64,128]{1,0:T(8,128)} copy-done((f32[64,128]{1,0:T(8,128)}, f32[64,128]{1,0:T(8,128)S(1)}, u32[]{:S(2)}) %copy-start.2) | copy-done | bytes 32792
  38.6 0.0 copy-start.3
  38.6 0.6 %copy-done.3 = f32[2,9,2,8]{3,2,1,0:T(2,128)} copy-done((f32[2,9,2,8]{3,2,1,0:T(2,128)}, f32[2,9,2,8]{3,2,1,0:T(2,128)S(1)}, u32[]{:S(2)}) %copy-start.3) | copy-done | bytes 1176
  39.2 2.6 %shard_map.75 = (f32[1024,128]{1,0:T(8,128)}, f32[64,128]{1,0:T(8,128)}, f32[1,1]{1,0:T(1,128)}, f32[2,9,8,32]{3,2,1,0:T(8,128)}, f32[2,9,2,8]{3,2,1,0:T(2,128)}) custom-call(f32[1024,128]{1,0:T(8,128)} %copy-done, f32[64,128]{1,0:T(8,128)} %copy-done.2, f32[1,1]{1,0:T(1,128)} %get-tuple-element.17.refs_2_, f32[2,9,8,32]{3,2,1,0:T(8,128)} %copy-done.1, ...), custom_call_target="tpu_custom_call" | custom-call | tf_op jit(solution)/shard_map/pallas_call | solution.py:492
  (12 shorter events, 0.2 us)
Async XLA Ops:
  0.6 0.7 %copy-start.6 = (bf16[2,2,8,3,3]{2,1,4,3,0:T(2,128)(2,1)S(1)}, bf16[2,2,8,3,3]{2,1,4,3,0:T(2,128)(2,1)}, u32[]{:S(2)}) copy-start(bf16[2,2,8,3,3]{2,1,4,3,0:T(2,128)(2,1)} %param.5) | copy-start | bytes 1732
  0.6 1.1 %copy-start.4 = (bf16[1,64,2,1024]{3,2,1,0:T(2,128)(2,1)S(1)}, bf16[1,64,2,1024]{3,2,1,0:T(2,128)(2,1)}, u32[]{:S(2)}) copy-start(bf16[1,64,2,1024]{3,2,1,0:T(2,128)(2,1)} %param.3) | copy-start | bytes 786436
  1.7 0.8 %copy-start.5 = (bf16[2,8,32,3,3]{2,1,4,3,0:T(8,128)(2,1)S(1)}, bf16[2,8,32,3,3]{2,1,4,3,0:T(8,128)(2,1)}, u32[]{:S(2)}) copy-start(bf16[2,8,32,3,3]{2,1,4,3,0:T(8,128)(2,1)} %param.4) | copy-start | bytes 27652
  36.6 0.8 %copy-start = (f32[1024,128]{1,0:T(8,128)}, f32[1024,128]{1,0:T(8,128)S(1)}, u32[]{:S(2)}) copy-start(f32[1024,128]{1,0:T(8,128)S(1)} %get-tuple-element.15.refs_0_) | copy-start | bytes 1572868
  37.4 0.6 %copy-start.1 = (f32[2,9,8,32]{3,2,1,0:T(8,128)}, f32[2,9,8,32]{3,2,1,0:T(8,128)S(1)}, u32[]{:S(2)}) copy-start(f32[2,9,8,32]{3,2,1,0:T(8,128)S(1)} %get-tuple-element.18.refs_3_) | copy-start | bytes 55300
  38.0 0.6 %copy-start.2 = (f32[64,128]{1,0:T(8,128)}, f32[64,128]{1,0:T(8,128)S(1)}, u32[]{:S(2)}) copy-start(f32[64,128]{1,0:T(8,128)S(1)} %get-tuple-element.16.refs_1_) | copy-start | bytes 98308
  38.6 0.6 %copy-start.3 = (f32[2,9,2,8]{3,2,1,0:T(2,128)}, f32[2,9,2,8]{3,2,1,0:T(2,128)S(1)}, u32[]{:S(2)}) copy-start(f32[2,9,2,8]{3,2,1,0:T(2,128)S(1)} %get-tuple-element.19.refs_4_) | copy-start | bytes 3460

commit v3 on v2

--- a/solution.py
+++ b/solution.py
@@ -82,16 +82,15 @@
 
 def flow_kernel(
     slabs, shards, window, own_fine, own_coarse, site_count,
-    x_ref, wa_ref, wb_ref,
+    field_ref, fine_in, coarse_in,
     out_ref, coarse_ref, dens_ref, fine_ref, cgrad_ref,
-    wa_buf, wb_buf, halo0, halo1, c1_ref, tiles0, tiles1, tilesb,
+    field_buf, fine_buf, coarse_buf, spaced, x_ref, c0_ref, k_buf, w_ref, cw_ref, halo0, halo1, c1_ref, tiles0, tiles1, tilesb,
     lat_ref, bend0, bend1, pool_buf, slope_ref, shalo,
     sa_ref, sb_ref, ra_buf, rb_buf, aa_buf, ab_buf,
-    send_sem, recv_sem,
+    load_sem, send_sem, recv_sem,
 ):
     half = x_ref.shape[1] // 2
-    deep = wb_ref.shape[0] - 2 * half
-    mc = deep // 4
+    mc = coarse_buf.shape[3]
     cc = 2 * mc
     patch = 9 * half
     three = 3 * half
@@ -104,6 +103,14 @@
     above = lax.rem(me + slabs - 1, slabs)
     below = lax.rem(me + 1, slabs)
 
+    loads = [
+        pltpu.make_async_copy(fine_in, fine_buf, load_sem.at[0]),
+        pltpu.make_async_copy(coarse_in, coarse_buf, load_sem.at[1]),
+        pltpu.make_async_copy(field_ref, field_buf, load_sem.at[2]),
+    ]
+    for load in loads:
+        load.start()
+
     barrier = pltpu.get_barrier_semaphore()
     for step in range(1, slabs):
         pl.semaphore_signal(
@@ -113,6 +120,24 @@
         pl.semaphore_signal(
             barrier, inc=1, device_id={"dp": lax.rem(mine + step, shards)}, device_id_type=MESH
         )
+    k_buf[mine] = jnp.zeros(k_buf.shape[1:], F32)
+    loads[0].wait()
+    loads[1].wait()
+    for l in range(2):
+        for k in range(9):
+            k_buf[mine, l, 0:own_fine, half * k : half * (k + 1)] = fine_buf[l, k].astype(F32)
+            k_buf[mine, l, 0:own_coarse, patch + mc * k : patch + mc * (k + 1)] = coarse_buf[
+                l, k
+            ].astype(F32)
+    loads[2].wait()
+    spaced[...] = field_buf[...].astype(F32)
+    tiles = x_ref.shape[2] // LANES
+    for i in range(2):
+        for b in range(tiles):
+            x_ref[i, :, LANES * b : LANES * (b + 1)] = spaced[
+                pl.ds(2 * b + i, 2 * half, stride=2 * tiles), :
+            ]
+        c0_ref[i] = x_ref[i, 0:half].astype(BF16)
     pl.semaphore_wait(barrier, slabs + shards - 2)
 
     used = [0]
@@ -133,21 +158,42 @@
         started.append(copy)
         return copy
 
-    wa_copies, wb_copies = [], []
-    for step in range(1, shards):
-        peer = lax.rem(mine + step, shards)
-        wa_copies.append(send(wa_ref, wa_buf.at[step - 1], {"dp": peer}))
-    from_above = send(x_ref.at[1, 0:half], halo0.at[0], {"slab": below})
-    from_below = send(x_ref.at[0, 0:half], halo0.at[1], {"slab": above})
-    for step in range(1, shards):
-        peer = lax.rem(mine + step, shards)
-        wb_copies.append(send(wb_ref, wb_buf.at[step - 1], {"dp": peer}))
+    def to_all(gathered, axis, place, count):
+        indices = []
+        for step in range(1, count):
+            indices.append(used[0])
+            send(gathered.at[place], gathered.at[place], {axis: lax.rem(place + step, count)})
+        return indices
+
+    def from_all(gathered, axis, place, count, indices):
+        for step in range(1, count):
+            source = lax.rem(place - step + count, count)
+            pltpu.make_async_remote_copy(
+                src_ref=gathered.at[place],
+                dst_ref=gathered.at[source],
+                send_sem=send_sem.at[indices[step - 1]],
+                recv_sem=recv_sem.at[indices[step - 1]],
+                device_id={axis: source},
+                device_id_type=MESH,
+            ).wait_recv()
+
+    k_copies = to_all(k_buf, "dp", mine, shards)
+    from_above = send(c0_ref.at[1], halo0.at[0], {"slab": below})
+    from_below = send(c0_ref.at[0], halo0.at[1], {"slab": above})
 
     sa_ref[...] = jnp.zeros_like(sa_ref)
     sb_ref[...] = jnp.zeros_like(sb_ref)
 
     def set_tile(tiles, index, rows, turn):
         tiles[three * index : three * (index + 1), :] = turn(rows).astype(BF16)
+
+    def turned_over(value, count, start):
+        filler = jnp.zeros((LANES - value.shape[0], value.shape[1]), F32)
+        flipped = jnp.transpose(jnp.concatenate([value, filler], axis=0))
+        parts = [
+            flipped[start + count * k : start + count * (k + 1), 0:count] for k in range(9)
+        ]
+        return jnp.concatenate(parts, axis=1)
 
     def own_terms(weight, tiles, first, second):
         stacked = jnp.concatenate(
@@ -158,10 +204,12 @@
 
     for i in range(2):
         set_tile(tiles0, i + 1, x_ref[i, 0:half].astype(F32), columns_forward)
-    total = wa_ref[...].astype(F32)
-    for step in range(1, shards):
-        wa_copies[step - 1].wait_recv()
-        total = total + wa_buf[step - 1].astype(F32)
+    from_all(k_buf, "dp", mine, shards, k_copies)
+    for d in range(shards):
+        for l in range(2):
+            w_ref[l, own_fine * d : own_fine * (d + 1)] = k_buf[d, l, 0:own_fine]
+            cw_ref[l, own_coarse * d : own_coarse * (d + 1)] = k_buf[d, l, 0:own_coarse, tail:]
+    total = w_ref[0]
     sums = own_terms(total, tiles0, three, 0)
     edges = [total[:, 0:three].astype(BF16), total[:, 2 * three : patch].astype(BF16)]
     from_above.wait_recv()
@@ -183,18 +231,15 @@
         set_tile(tiles1, i + 1, c1_ref[i].astype(F32), columns_forward)
         moved = lat_ref[i, half:]
         density = density + moved * moved
-    total = wb_ref[...].astype(F32)
-    for step in range(1, shards):
-        wb_copies[step - 1].wait_recv()
-        total = total + wb_buf[step - 1].astype(F32)
-    weight1 = total[0:half]
-    back1 = total[half : 2 * half]
+    weight1 = w_ref[1]
     sums = own_terms(weight1, tiles1, three, 0)
     edges = [weight1[:, 0:three].astype(BF16), weight1[:, 2 * three : patch].astype(BF16)]
     coarse_weights = total[2 * half :, 0:cpatch]
     cfor0, cfor1, cback1, cback0 = [
         coarse_weights[mc * k : mc * (k + 1)].astype(BF16) for k in range(4)
     ]
+    back1 = turned_over(w_ref[1], half, 0)
+    cback0, cback1 = [turned_over(cw_ref[l], mc, inset).astype(BF16) for l in range(2)]
     from_above.wait_recv()
     set_tile(tiles1, 0, halo1[0].astype(F32), columns_forward)
     from_below.wait_recv()
@@ -223,7 +268,6 @@
         slope_ref[i, cc:half] = (lat_ref[i, cc:half] * inverse * bend1[i, cc:half]).astype(BF16)
     high_above = send(slope_ref.at[1, cc:half], shalo.at[0, cc:half], {"slab": below})
     high_below = send(slope_ref.at[0, cc:half], shalo.at[1, cc:half], {"slab": above})
-    tiles = x_ref.shape[2] // LANES
     for i in range(2):
         moved = lat_ref[i, 0:half]
         density = density + moved * moved
@@ -233,6 +277,8 @@
             ]
     for copy in pool_copies:
         copy.wait_recv()
+
+    cfor0, cfor1 = [cw_ref[l, :, inset : inset + cpatch].astype(BF16) for l in range(2)]
 
     width = pool_buf.shape[2]
 
@@ -347,14 +393,6 @@
         peer = lax.rem(mine + step, shards)
         ra_copies.append(send(sa_ref.at[peer], ra_buf.at[step - 1], {"dp": peer}))
 
-    def over_slabs(gathered):
-        copies = []
-        for step in range(1, slabs):
-            peer = lax.rem(me + step, slabs)
-            copies.append(used[0])
-            send(gathered.at[me], gathered.at[me], {"slab": peer})
-        return copies
-
     block = sb_ref[mine]
     for step in range(1, shards):
         rb_copies[step - 1].wait_recv()
@@ -362,27 +400,15 @@
     row = lax.broadcasted_iota(jnp.int32, block.shape, 0)
     lane = lax.broadcasted_iota(jnp.int32, block.shape, 1)
     ab_buf[me] = jnp.where((row == 2 * own_coarse) & (lane == patch), site_density, block)
-    ab_copies = over_slabs(ab_buf)
+    ab_copies = to_all(ab_buf, "slab", me, slabs)
     block = sa_ref[mine]
     for step in range(1, shards):
         ra_copies[step - 1].wait_recv()
         block = block + ra_buf[step - 1]
     aa_buf[me] = block
-    aa_copies = over_slabs(aa_buf)
-
-    def wait_slabs(gathered, copies):
-        for step in range(1, slabs):
-            source = lax.rem(me - step + slabs, slabs)
-            pltpu.make_async_remote_copy(
-                src_ref=gathered.at[me],
-                dst_ref=gathered.at[source],
-                send_sem=send_sem.at[copies[step - 1]],
-                recv_sem=recv_sem.at[copies[step - 1]],
-                device_id={"slab": source},
-                device_id_type=MESH,
-            ).wait_recv()
-
-    wait_slabs(ab_buf, ab_copies)
+    aa_copies = to_all(aa_buf, "slab", me, slabs)
+
+    from_all(ab_buf, "slab", me, slabs, ab_copies)
     block = ab_buf[0]
     for s in range(1, slabs):
         block = block + ab_buf[s]
@@ -393,7 +419,7 @@
             cgrad_ref[l, k] = block[
                 own_coarse * l : own_coarse * (l + 1), patch + mc * k : patch + mc * (k + 1)
             ]
-    wait_slabs(aa_buf, aa_copies)
+    from_all(aa_buf, "slab", me, slabs, aa_copies)
     block = aa_buf[0]
     for s in range(1, slabs):
         block = block + aa_buf[s]
@@ -414,7 +440,6 @@
 
 def on_device(lattice_field, fine_kernels, coarse_kernels):
     slabs, shards = lax.axis_size("slab"), lax.axis_size("dp")
-    mine = lax.axis_index("dp")
     _, channels, height, cols = lattice_field.shape
     _, own_fine, half, _, _ = fine_kernels.shape
     _, own_coarse, mc, _, _ = coarse_kernels.shape
@@ -424,27 +449,14 @@
     site_count = height * slabs * cols
     window = min(slabs, 9)
 
-    def embedded(kernel, own):
-        count = own * shards
-        tiled = jnp.tile(kernel, (1, shards, 1, 1, 1))
-        owner = lax.broadcasted_iota(jnp.int32, (1, count, 1, 1, 1), 1) // own
-        full = jnp.where(owner == mine, tiled, jnp.zeros_like(tiled))
-        forward = jnp.transpose(full, (0, 1, 3, 4, 2)).reshape(2, count, -1)
-        backward = jnp.transpose(full, (0, 2, 3, 4, 1)).reshape(2, count, -1)
-        pads = ((0, 0), (0, 0), (0, padded - forward.shape[2]))
-        return jnp.pad(forward, pads), jnp.pad(backward, pads)
-
-    forward, backward = embedded(fine_kernels, own_fine)
-    cforward, cbackward = embedded(coarse_kernels, own_coarse)
-    wa = forward[0]
-    wb = jnp.concatenate(
-        [forward[1], backward[1], cforward[0], cforward[1], cbackward[1], cbackward[0]], axis=0
-    )
-    x = jnp.transpose(lattice_field[0], (1, 0, 2))
+    field = lattice_field.reshape(channels, height, cols // LANES, LANES)
+    field = jnp.transpose(field, (0, 2, 1, 3)).reshape(-1, LANES)
+    fine_in = jnp.transpose(fine_kernels, (0, 3, 4, 1, 2)).reshape(2, 9, own_fine, half)
+    coarse_in = jnp.transpose(coarse_kernels, (0, 3, 4, 1, 2)).reshape(2, 9, own_coarse, mc)
 
     pad_fine = round_up(own_fine, 8)
     tall = channels * height * cols // LANES
-    copies = 4 * (shards - 1) + 8 + (window - 1) + 2 * (slabs - 1)
+    copies = 3 * (shards - 1) + 8 + (window - 1) + 2 * (slabs - 1)
     vmem = pl.BlockSpec(memory_space=pltpu.VMEM)
     shapes = (
         jax.ShapeDtypeStruct((tall, LANES), F32),
@@ -458,11 +470,18 @@
             flow_kernel, slabs, shards, window, own_fine, own_coarse, site_count
         ),
         out_shape=shapes,
-        in_specs=[vmem] * 3,
+        in_specs=[pl.BlockSpec(memory_space=pltpu.HBM)] * 3,
         out_specs=(vmem,) * 5,
         scratch_shapes=[
-            pltpu.VMEM((shards - 1,) + wa.shape, BF16),
-            pltpu.VMEM((shards - 1,) + wb.shape, BF16),
+            pltpu.VMEM(field.shape, BF16),
+            pltpu.VMEM(fine_in.shape, BF16),
+            pltpu.VMEM(coarse_in.shape, BF16),
+            pltpu.VMEM(field.shape, F32),
+            pltpu.VMEM((2, channels, cols), F32),
+            pltpu.VMEM((2, half, cols), BF16),
+            pltpu.VMEM((shards, 2, pad_fine, padded), F32),
+            pltpu.VMEM((2, half, padded), F32),
+            pltpu.VMEM((2, mc, LANES), F32),
             pltpu.VMEM((2, half, cols), BF16),
             pltpu.VMEM((2, half, cols), BF16),
             pltpu.VMEM((2, half, cols), BF16),
@@ -481,21 +500,23 @@
             pltpu.VMEM((shards - 1, pad_fine, padded), F32),
             pltpu.VMEM((slabs, pad_fine, padded), F32),
             pltpu.VMEM((slabs, pad_fine, padded), F32),
+            pltpu.SemaphoreType.DMA((3,)),
             pltpu.SemaphoreType.DMA((copies,)),
             pltpu.SemaphoreType.DMA((copies,)),
         ],
         compiler_params=pltpu.CompilerParams(
             collective_id=0, has_side_effects=True, vmem_limit_bytes=40 * 1024 * 1024
         ),
-    )(x, wa, wb)
-
+    )(field, fine_in, coarse_in)
     lat, coarse, dens, fine, coarse_grads = pl.pallas_call(
         store_kernel,
         out_shape=shapes,
-        in_specs=[vmem] * 5,
-        out_specs=(pl.BlockSpec(memory_space=pl.ANY),) * 5,
+        in_specs=[pl.BlockSpec(memory_space=pl.ANY)] * 5,
+        out_specs=(pl.BlockSpec(memory_space=pltpu.HBM),) * 5,
         scratch_shapes=[pltpu.SemaphoreType.DMA((5,))],
+        compiler_params=pltpu.CompilerParams(vmem_limit_bytes=1024 * 1024),
     )(*results)
+
     lat = jnp.transpose(lat.reshape(channels, cols // LANES, height, LANES), (0, 2, 1, 3))
     return (
         lat.reshape(1, channels, height, cols),

time: 42 us -> 38.6 us (0.919)
  local copies, waits for them, and re-layouts: 4.69 us -> 2.41 us
  Pallas kernels: 36.1 us -> 35.2 us
    unnamed x20 -> x6, local copies, waits for them, and re-layouts: 4.08 us -> 2.41 us
    pallas_call x1, Pallas kernels: 2.55 us -> 1.48 us  [on_device(): pl.pallas_call(store_kernel, out_shape=shapes, in_specs=[pl.BlockSpec(mem...]
    reshape x4 -> x0, local copies, waits for them, and re-layouts: 0.45 us -> none  [the longest x2 0.24 us: embedded(): forward = jnp.transpose(full, (0, 1, 3, 4, 2)).reshape(2, count, -1)]
where the time goes in v3:
time: 38.6 us; the launch traced here: 38.3 us
  Pallas kernels  35.2 us (91%)
  local copies, waits for them, and re-layouts  2.41 us (6%)
  between operations  0.65 us (2%)
    pallas_call x1, Pallas kernels, on_device(): pl.pallas_call(functools.partial(flow_kernel, slabs, shards, window, own_...  33.8 us
    unnamed x6, local copies, waits for them, and re-layouts  2.41 us
    pallas_call x1, Pallas kernels, on_device(): pl.pallas_call(store_kernel, out_shape=shapes, in_specs=[pl.BlockSpec(mem...  1.48 us

profile of v3, /device:TPU:0, one launch (start us, length us, event | category | flops | bytes accessed | tf_op | source)
XLA Modules:
  0.0 38.3 jit_solution(16886521001344687432)
XLA Ops:
  0.6 0.0 copy-start
  0.6 0.9 %copy-done = bf16[1,64,2,1024]{3,2,1,0:T(2,128)(2,1)S(1)} copy-done((bf16[1,64,2,1024]{3,2,1,0:T(2,128)(2,1)S(1)}, bf16[1,64,2,1024]{3,2,1,0:T(2,128)(2,1)}, u32[]{:S(2)}) %copy-start) | copy-done | bytes 262168
  1.6 0.0 copy-start.1
  1.6 0.8 %copy-done.1 = bf16[2,8,32,3,3]{2,1,4,3,0:T(8,128)(2,1)S(1)} copy-done((bf16[2,8,32,3,3]{2,1,4,3,0:T(8,128)(2,1)S(1)}, bf16[2,8,32,3,3]{2,1,4,3,0:T(8,128)(2,1)}, u32[]{:S(2)}) %copy-start.1) | copy-done | bytes 9240
  2.4 0.0 copy-start.2
  2.4 0.7 %copy-done.2 = bf16[2,2,8,3,3]{2,1,4,3,0:T(2,128)(2,1)S(1)} copy-done((bf16[2,2,8,3,3]{2,1,4,3,0:T(2,128)(2,1)S(1)}, bf16[2,2,8,3,3]{2,1,4,3,0:T(2,128)(2,1)}, u32[]{:S(2)}) %copy-start.2) | copy-done | bytes 600
  3.1 33.8 %shard_map.74 = (f32[1024,128]{1,0:T(8,128)S(1)}, f32[64,128]{1,0:T(8,128)S(1)}, f32[1,1]{1,0:T(1,128)}, f32[2,9,8,32]{3,2,1,0:T(8,128)S(1)}, f32[2,9,2,8]{3,2,1,0:T(2,128)S(1)}) custom-call(bf16[1024,128]{1,0:T(8,128)(2,1)S(1)} %bitcast.24, bf16[2,9,8,32]{3,2,1,0:T(8,128)(2,1)S(1)} %bitcast.25, bf16[2,9,2,8]{3,2,1,0:T(2,128)(2,1)S(1)} %bitcast.26), custom_call_target="tpu_custom_call" | custom-call | tf_op jit(solution)/shard_map/pallas_call | solution.py:468
  36.8 1.5 %shard_map.75 = (f32[1024,128]{1,0:T(8,128)}, f32[64,128]{1,0:T(8,128)}, f32[1,1]{1,0:T(1,128)}, f32[2,9,8,32]{3,2,1,0:T(8,128)}, f32[2,9,2,8]{3,2,1,0:T(2,128)}) custom-call(f32[1024,128]{1,0:T(8,128)S(1)} %get-tuple-element.15.refs_0_, f32[64,128]{1,0:T(8,128)S(1)} %get-tuple-element.16.refs_1_, f32[1,1]{1,0:T(1,128)} %get-tuple-element.17.refs_2_, ...), custom_call_target="tpu_custom_call" | custom-call | tf_op jit(solution)/shard_map/pallas_call | solution.py:511
Async XLA Ops:
  0.6 1.0 %copy-start = (bf16[1,64,2,1024]{3,2,1,0:T(2,128)(2,1)S(1)}, bf16[1,64,2,1024]{3,2,1,0:T(2,128)(2,1)}, u32[]{:S(2)}) copy-start(bf16[1,64,2,1024]{3,2,1,0:T(2,128)(2,1)} %param.3) | copy-start | bytes 786436
  1.6 0.8 %copy-start.1 = (bf16[2,8,32,3,3]{2,1,4,3,0:T(8,128)(2,1)S(1)}, bf16[2,8,32,3,3]{2,1,4,3,0:T(8,128)(2,1)}, u32[]{:S(2)}) copy-start(bf16[2,8,32,3,3]{2,1,4,3,0:T(8,128)(2,1)} %param.4) | copy-start | bytes 27652
  2.4 0.7 %copy-start.2 = (bf16[2,2,8,3,3]{2,1,4,3,0:T(2,128)(2,1)S(1)}, bf16[2,2,8,3,3]{2,1,4,3,0:T(2,128)(2,1)}, u32[]{:S(2)}) copy-start(bf16[2,2,8,3,3]{2,1,4,3,0:T(2,128)(2,1)} %param.5) | copy-start | bytes 1732

commit v4 on v3

--- a/solution.py
+++ b/solution.py
@@ -85,7 +85,7 @@
     field_ref, fine_in, coarse_in,
     out_ref, coarse_ref, dens_ref, fine_ref, cgrad_ref,
     field_buf, fine_buf, coarse_buf, spaced, x_ref, c0_ref, k_buf, w_ref, cw_ref, halo0, halo1, c1_ref, tiles0, tiles1, tilesb,
-    lat_ref, bend0, bend1, pool_buf, slope_ref, shalo,
+    lat_ref, bend0, bend1, pool_buf, slope_ref, base_ref, shalo,
     sa_ref, sb_ref, ra_buf, rb_buf, aa_buf, ab_buf,
     load_sem, send_sem, recv_sem,
 ):
@@ -265,9 +265,12 @@
         pool_copies.append(send(pool_buf.at[0], pool_buf.at[k], {"slab": peer}))
     finish(slice(cc, half))
     for i in range(2):
-        slope_ref[i, cc:half] = (lat_ref[i, cc:half] * inverse * bend1[i, cc:half]).astype(BF16)
-    high_above = send(slope_ref.at[1, cc:half], shalo.at[0, cc:half], {"slab": below})
-    high_below = send(slope_ref.at[0, cc:half], shalo.at[1, cc:half], {"slab": above})
+        base = (lat_ref[i, 0:half] * inverse * bend1[i]).astype(BF16)
+        base_ref[i, 0:half] = base
+        base_ref[i, half:] = bend1[i, 0:cc].astype(BF16)
+        slope_ref[i, cc:half] = base[cc:half]
+    from_above = send(base_ref.at[1], shalo.at[0], {"slab": below})
+    from_below = send(base_ref.at[0], shalo.at[1], {"slab": above})
     for i in range(2):
         moved = lat_ref[i, 0:half]
         density = density + moved * moved
@@ -330,15 +333,24 @@
     grad_high = high * inverse + product(cback1, back_patches.astype(BF16))
     slope_c0 = (grad_high * (1.0 - bent_c0 * bent_c0)).astype(BF16)
     kernel_c0 = coarse_kernel_grad(slope_c0, patches0)
-    back_patches = coarse_patches(cut(slope_c0.astype(F32)), columns_backward, -1, [0])
-    grad_own = grad_low[:, 0:width] + product(cback0, back_patches.astype(BF16))
-    pooled_grad = jnp.concatenate([grad_own, grad_high[:, 0:width]], axis=0) - pooled * inverse
-    spread = unpool_columns(pooled_grad)
+    wanted = [0, 1, window - 1]
+    back_patches = coarse_patches(cut(slope_c0.astype(F32)), columns_backward, -1, wanted)
+
+    def chosen(value):
+        pieces = cut(value)
+        return jnp.concatenate([pieces[k] for k in wanted], axis=1)
+
+    pooled_three = jnp.concatenate([pool_buf[k] for k in wanted], axis=1)
+    grad_three = chosen(grad_low) + product(cback0, back_patches.astype(BF16))
+    grad_three = jnp.concatenate([grad_three, chosen(grad_high)], axis=0)
+    spread_three = unpool_columns(grad_three - pooled_three * inverse)
+    cols = x_ref.shape[2]
+    spread, spread_below, spread_above = [
+        spread_three[:, cols * k : cols * (k + 1)] for k in range(3)
+    ]
 
     for i in range(2):
         slope_ref[i, 0:cc] = ((lat_ref[i, 0:cc] * inverse + spread) * bend1[i, 0:cc]).astype(BF16)
-    low_above = send(slope_ref.at[1, 0:cc], shalo.at[0, 0:cc], {"slab": below})
-    low_below = send(slope_ref.at[0, 0:cc], shalo.at[1, 0:cc], {"slab": above})
     kernel_1 = product_nt(slope_ref[0], tiles1[0:patch, :])
     kernel_1 = kernel_1 + product_nt(slope_ref[1], tiles1[three : three + patch, :])
     for d in range(shards):
@@ -369,12 +381,14 @@
     sums = own_terms(back1, tilesb, 0, three)
     edges = [back1[:, 2 * three : patch].astype(BF16), back1[:, 0:three].astype(BF16)]
 
-    high_above.wait_recv()
-    low_above.wait_recv()
-    set_tile(tilesb, 3, shalo[0].astype(F32), columns_backward)
-    high_below.wait_recv()
-    low_below.wait_recv()
-    set_tile(tilesb, 0, shalo[1].astype(F32), columns_backward)
+    def edge_slope(index, addition):
+        low = shalo[index, 0:cc].astype(F32) + addition * shalo[index, half:].astype(F32)
+        return jnp.concatenate([rounded(low), shalo[index, cc:half].astype(F32)], axis=0)
+
+    from_above.wait_recv()
+    set_tile(tilesb, 3, edge_slope(0, spread_above), columns_backward)
+    from_below.wait_recv()
+    set_tile(tilesb, 0, edge_slope(1, spread_below), columns_backward)
     kernel_0 = None
     for i in range(2):
         edge = three * 3 * (1 - i)
@@ -447,7 +461,7 @@
     patch, cpatch = 9 * half, 9 * mc
     padded = round_up(patch, LANES)
     site_count = height * slabs * cols
-    window = min(slabs, 9)
+    window = min(slabs, 11)
 
     field = lattice_field.reshape(channels, height, cols // LANES, LANES)
     field = jnp.transpose(field, (0, 2, 1, 3)).reshape(-1, LANES)
@@ -456,7 +470,7 @@
 
     pad_fine = round_up(own_fine, 8)
     tall = channels * height * cols // LANES
-    copies = 3 * (shards - 1) + 8 + (window - 1) + 2 * (slabs - 1)
+    copies = 3 * (shards - 1) + 6 + (window - 1) + 2 * (slabs - 1)
     vmem = pl.BlockSpec(memory_space=pltpu.VMEM)
     shapes = (
         jax.ShapeDtypeStruct((tall, LANES), F32),
@@ -493,7 +507,8 @@
             pltpu.VMEM((2, half, cols), F32),
             pltpu.VMEM((window, cc, width), F32),
             pltpu.VMEM((2, half, cols), BF16),
-            pltpu.VMEM((2, half, cols), BF16),
+            pltpu.VMEM((2, half + cc, cols), BF16),
+            pltpu.VMEM((2, half + cc, cols), BF16),
             pltpu.VMEM((shards, pad_fine, padded), F32),
             pltpu.VMEM((shards, pad_fine, padded), F32),
             pltpu.VMEM((shards - 1, pad_fine, padded), F32),

time: 38.6 us -> 35.8 us (0.927)
  Pallas kernels: 35.2 us -> 32.4 us
    pallas_call x1, Pallas kernels: 33.8 us -> 31 us  [on_device(): pl.pallas_call(functools.partial(flow_kernel, slabs, shards, window, own_...]
where the time goes in v4:
time: 35.8 us; the launch traced here: 35.5 us
  Pallas kernels  32.4 us (91%)
  local copies, waits for them, and re-layouts  2.41 us (7%)
  between operations  0.65 us (2%)
    pallas_call x1, Pallas kernels, on_device(): pl.pallas_call(functools.partial(flow_kernel, slabs, shards, window, own_...  31 us
    unnamed x6, local copies, waits for them, and re-layouts  2.41 us
    pallas_call x1, Pallas kernels, on_device(): pl.pallas_call(store_kernel, out_shape=shapes, in_specs=[pl.BlockSpec(mem...  1.48 us

profile of v4, /device:TPU:0, one launch (start us, length us, event | category | flops | bytes accessed | tf_op | source)
XLA Modules:
  0.0 35.5 jit_solution(6788594828692806554)
XLA Ops:
  0.6 0.0 copy-start
  0.6 0.9 %copy-done = bf16[1,64,2,1024]{3,2,1,0:T(2,128)(2,1)S(1)} copy-done((bf16[1,64,2,1024]{3,2,1,0:T(2,128)(2,1)S(1)}, bf16[1,64,2,1024]{3,2,1,0:T(2,128)(2,1)}, u32[]{:S(2)}) %copy-start) | copy-done | bytes 262168
  1.6 0.0 copy-start.1
  1.6 0.8 %copy-done.1 = bf16[2,8,32,3,3]{2,1,4,3,0:T(8,128)(2,1)S(1)} copy-done((bf16[2,8,32,3,3]{2,1,4,3,0:T(8,128)(2,1)S(1)}, bf16[2,8,32,3,3]{2,1,4,3,0:T(8,128)(2,1)}, u32[]{:S(2)}) %copy-start.1) | copy-done | bytes 9240
  2.4 0.0 copy-start.2
  2.4 0.7 %copy-done.2 = bf16[2,2,8,3,3]{2,1,4,3,0:T(2,128)(2,1)S(1)} copy-done((bf16[2,2,8,3,3]{2,1,4,3,0:T(2,128)(2,1)S(1)}, bf16[2,2,8,3,3]{2,1,4,3,0:T(2,128)(2,1)}, u32[]{:S(2)}) %copy-start.2) | copy-done | bytes 600
  3.1 31.0 %shard_map.74 = (f32[1024,128]{1,0:T(8,128)S(1)}, f32[64,128]{1,0:T(8,128)S(1)}, f32[1,1]{1,0:T(1,128)}, f32[2,9,8,32]{3,2,1,0:T(8,128)S(1)}, f32[2,9,2,8]{3,2,1,0:T(2,128)S(1)}) custom-call(bf16[1024,128]{1,0:T(8,128)(2,1)S(1)} %bitcast.24, bf16[2,9,8,32]{3,2,1,0:T(8,128)(2,1)S(1)} %bitcast.25, bf16[2,9,2,8]{3,2,1,0:T(2,128)(2,1)S(1)} %bitcast.26), custom_call_target="tpu_custom_call" | custom-call | tf_op jit(solution)/shard_map/pallas_call | solution.py:482
  34.0 1.5 %shard_map.75 = (f32[1024,128]{1,0:T(8,128)}, f32[64,128]{1,0:T(8,128)}, f32[1,1]{1,0:T(1,128)}, f32[2,9,8,32]{3,2,1,0:T(8,128)}, f32[2,9,2,8]{3,2,1,0:T(2,128)}) custom-call(f32[1024,128]{1,0:T(8,128)S(1)} %get-tuple-element.15.refs_0_, f32[64,128]{1,0:T(8,128)S(1)} %get-tuple-element.16.refs_1_, f32[1,1]{1,0:T(1,128)} %get-tuple-element.17.refs_2_, ...), custom_call_target="tpu_custom_call" | custom-call | tf_op jit(solution)/shard_map/pallas_call | solution.py:526
Async XLA Ops:
  0.6 1.0 %copy-start = (bf16[1,64,2,1024]{3,2,1,0:T(2,128)(2,1)S(1)}, bf16[1,64,2,1024]{3,2,1,0:T(2,128)(2,1)}, u32[]{:S(2)}) copy-start(bf16[1,64,2,1024]{3,2,1,0:T(2,128)(2,1)} %param.3) | copy-start | bytes 786436
  1.6 0.8 %copy-start.1 = (bf16[2,8,32,3,3]{2,1,4,3,0:T(8,128)(2,1)S(1)}, bf16[2,8,32,3,3]{2,1,4,3,0:T(8,128)(2,1)}, u32[]{:S(2)}) copy-start(bf16[2,8,32,3,3]{2,1,4,3,0:T(8,128)(2,1)} %param.4) | copy-start | bytes 27652
  2.4 0.7 %copy-start.2 = (bf16[2,2,8,3,3]{2,1,4,3,0:T(2,128)(2,1)S(1)}, bf16[2,2,8,3,3]{2,1,4,3,0:T(2,128)(2,1)}, u32[]{:S(2)}) copy-start(bf16[2,2,8,3,3]{2,1,4,3,0:T(2,128)(2,1)} %param.5) | copy-start | bytes 1732
